TPU v7x, 128 devices: a whole 4x4x4 slice. The times are simulated.
128 devices in a mesh: gx: 16 (over z, y), gy: 8 (over x, core).
Axes of the slice: x: 4, y: 4, z: 4, core: 2. Of those that a mesh axis runs over, the one named last changes fastest.
Arguments:
- populations: float32 [19, 512, 6144], P(None, 'gy', 'gx'), may hold values from 0 to 0.5, as said below
- heights: int32 [2, 512, 1536], replicated, may hold values from 0 to 4
- wall_class: int32 [512, 1536], replicated, may hold values from 0 to 3
- wetting: float32 [4], replicated, may hold values from -0.3 to 0.3
- owner: int32 [8, 16, 6], replicated, may hold values from -1 to 15, as said below
Outputs:
- stepped: float32 [8, 64, 19, 32, 128], P('gy', 'gx')
Inputs may be any that keep to these rules, and one draw needn't show every extreme that they name: `populations`: each population is w_i times a factor between 0.5 and 1.5. `owner`: each row of gy holds between 49 and 64 active blocks; in each row, every receiver gets at most 4 blocks and some receiver exactly 4; no device's blocks go twice to one receiver.
All inputs are finite; a program needn't handle non-finite values.
Results may differ from a plain program's by a relative error of at most 0.0003.
Values sent between devices are 32-bit elements; how exact they have to be, the bound alone decides.
No kernel may reach another device: no remote copies, remote signals or barrier semaphores. Data moves between devices by JAX's collectives and lax.ppermute only.
A program may use at most 128 MiB of HBM per device.

v0:
```python
import functools

import jax
import jax.numpy as jnp
import numpy as np
from jax import lax
from jax.experimental import pallas as pl
from jax.experimental.pallas import tpu as pltpu
from jax.sharding import PartitionSpec as P

B = 32
CZ = 4
BXD = 3
BYD = 2
CAP = 4
BLK = BXD * BYD
Q = 19
TILE = 8
LANES = 128
ROWS = 64
GROUPS = ROWS // TILE
SENT = [i for i in range(Q) if i != 17]
TAIL = 17
NDEV = 16
PIECE = BLK * (B + 4)
SLOTS = CAP * (B + 4)
BASE = 16
PADDED = ROWS + 2 * BASE

VELOCITY = [
    (0, 0, 0),
    (1, 0, 0),
    (-1, 0, 0),
    (0, 1, 0),
    (0, -1, 0),
    (0, 0, 1),
    (0, 0, -1),
    (1, 1, 0),
    (-1, -1, 0),
    (1, -1, 0),
    (-1, 1, 0),
    (1, 0, 1),
    (-1, 0, -1),
    (1, 0, -1),
    (-1, 0, 1),
    (0, 1, 1),
    (0, -1, -1),
    (0, 1, -1),
    (0, -1, 1),
]
WEIGHTS = [1.0 / 3.0] + [1.0 / 18.0] * 6 + [1.0 / 36.0] * 12
OPPOSITE = [0, 2, 1, 4, 3, 6, 5, 8, 7, 10, 9, 12, 11, 14, 13, 16, 15, 18, 17]
CARRIERS = (6, 12, 13)
FIXED_TOP = (6, 12, 13, 16)

f32 = jnp.float32
i32 = jnp.int32
VMEM_LIMIT = 32 * 1024 * 1024


def params(**more):
    return pltpu.CompilerParams(vmem_limit_bytes=VMEM_LIMIT, **more)


def lane_of():
    return lax.broadcasted_iota(i32, (TILE, LANES), 1)


def row_of():
    return lax.broadcasted_iota(i32, (TILE, LANES), 0)


def collide(f, gas):
    pairs = [(i, i + 1) for i in range(1, Q, 2)]
    total = {i: f[i] + f[o] for i, o in pairs}
    diff = {i: f[i] - f[o] for i, o in pairs}
    rho = f[0]
    for i, _ in pairs:
        rho = rho + total[i]
    jx = diff[1] + diff[7] + diff[9] + diff[11] + diff[13]
    jy = diff[3] + diff[7] - diff[9] + diff[15] + diff[17]
    jz = diff[5] + diff[11] - diff[13] + diff[15] - diff[17]
    inv = 1.0 / rho
    scaled = rho - 1.5 * inv * (jx * jx + jy * jy + jz * jz)
    along = {
        1: jx,
        3: jy,
        5: jz,
        7: jx + jy,
        9: jx - jy,
        11: jx + jz,
        13: jx - jz,
        15: jy + jz,
        17: jy - jz,
    }
    is_gas = gas > 0
    out = [None] * Q
    out[0] = jnp.where(
        is_gas, WEIGHTS[0] * gas, -0.6 * f[0] + (1.6 * WEIGHTS[0]) * scaled
    )
    for first, last in ((1, 5), (7, 17)):
        w = WEIGHTS[first]
        base = (1.6 * w) * scaled
        bend = (7.2 * w) * inv
        held = w * gas
        for i in range(first, last + 1, 2):
            cj = along[i]
            even = base + bend * (cj * cj) - 0.3 * total[i]
            odd = 0.25 * diff[i] + (1.5 * w) * cj
            out[i] = jnp.where(is_gas, held, even + odd)
            out[i + 1] = jnp.where(is_gas, held, even - odd)
    return out


def shifted(load, c, shift, lane):
    if shift == 0:
        return load(c)
    if shift > 0:
        here = load(c)
        if c > 0:
            here = jnp.where(lane >= LANES - shift, load(c - 1), here)
        return pltpu.roll(here, shift, 1)
    here = load(c)
    if c < 3:
        here = jnp.where(lane < -shift, load(c + 1), here)
    return pltpu.roll(here, LANES + shift, 1)


def pull(load, i, c, lane, extra):
    cx, cy, cz = VELOCITY[i]
    moved = shifted(lambda t: load(i, t, cy), c, 4 * cx + cz - extra, lane)
    if cz == 1:
        wall = shifted(lambda t: load(OPPOSITE[i], t, 0), c, -extra, lane)
        moved = jnp.where(lane % CZ == 0, wall, moved)
    elif cz == -1:
        moved = jnp.where(lane % CZ == CZ - 1, jnp.float32(WEIGHTS[i]), moved)
    return moved


def pack_rows_kernel(first_ref, last_ref, up_ref, down_ref):
    for i in range(Q):
        up_ref[2 * i : 2 * i + 2, :] = first_ref[i, 0:2, :]
        down_ref[2 * i : 2 * i + 2, :] = last_ref[i, TILE - 2 : TILE, :]


def pack_rows(populations):
    width = populations.shape[2]
    out = jax.ShapeDtypeStruct((2 * Q + 2, width), f32)
    return pl.pallas_call(
        pack_rows_kernel,
        grid=(1,),
        in_specs=[
            pl.BlockSpec((Q, TILE, width), lambda g: (0, 0, 0)),
            pl.BlockSpec((Q, TILE, width), lambda g: (0, GROUPS - 1, 0)),
        ],
        out_specs=[pl.BlockSpec((2 * Q + 2, width), lambda g: (0, 0))] * 2,
        out_shape=[out, out],
        compiler_params=params(),
        name="pack_rows",
    )(populations, populations)


def pack_cols_kernel(pop_ref, below_ref, above_ref, out_ref, halo_ref):
    lane = lane_of()
    for i in range(Q):
        packed = pop_ref[i, 0:TILE, :]
        for g in range(1, GROUPS):
            rolled = pltpu.roll(pop_ref[i, TILE * g : TILE * (g + 1), :], 16 * g, 1)
            packed = jnp.where(lane >= 16 * g, rolled, packed)
        out_ref[i] = packed
    halo_ref[...] = jnp.zeros(halo_ref.shape, f32)
    for i in range(Q):
        halo_ref[i, 0:2, :] = below_ref[2 * i : 2 * i + 2, :]
        halo_ref[i, TILE - 2 : TILE, :] = above_ref[2 * i : 2 * i + 2, :]
    for part in range(3):
        packed = halo_ref[8 * part]
        for g in range(1, 8):
            if 8 * part + g < Q:
                rolled = pltpu.roll(halo_ref[8 * part + g], 16 * g, 1)
                packed = jnp.where(lane >= 16 * g, rolled, packed)
        out_ref[Q + part] = packed


def pack_cols(populations, below, above):
    return pl.pallas_call(
        pack_cols_kernel,
        grid=(1,),
        in_specs=[
            pl.BlockSpec((Q, ROWS, LANES), lambda g: (0, 0, 0)),
            pl.BlockSpec((2 * Q + 2, LANES), lambda g: (0, 0)),
            pl.BlockSpec((2 * Q + 2, LANES), lambda g: (0, 0)),
        ],
        out_specs=pl.BlockSpec((Q + 3, TILE, LANES), lambda g: (0, 0, 0)),
        out_shape=jax.ShapeDtypeStruct((Q + 3, TILE, LANES), f32),
        scratch_shapes=[pltpu.VMEM((Q, TILE, LANES), f32)],
        compiler_params=params(),
        name="pack_cols",
    )(populations, below, above)


def own_kernel(
    pos_ref,
    owner_ref,
    wet_ref,
    pop_ref,
    h0_ref,
    h1_ref,
    ht0_ref,
    ht1_ref,
    hb0_ref,
    hb1_ref,
    k0_ref,
    k1_ref,
    kt0_ref,
    kt1_ref,
    kb0_ref,
    kb1_ref,
    post_ref,
    gas_ref,
    packed_ref,
):
    gy, gx = (pos_ref[0], pos_ref[1])
    offset = (gx * (BXD * B)) % LANES
    wide = 4 * LANES
    cell = lax.broadcasted_iota(i32, (2 * LANES, wide), 0)
    place = lax.broadcasted_iota(i32, (2 * LANES, wide), 1)
    spread = (cell == offset + place // CZ).astype(f32)

    def widen(left, right):
        both = jnp.concatenate([left, right], axis=1).astype(f32)
        return jnp.dot(both, spread, preferred_element_type=f32)

    def active(row, col, j):
        return (owner_ref[(row * NDEV + col) * BLK + j] >= 0).astype(f32)

    next_gx = (gx + 1) % NDEV

    def act_tile(row, by, c):
        return active(row, gx, BXD * by + c) if c < BXD else active(row, next_gx, BXD * by)

    def level_of(kind):
        value = wet_ref[0]
        value = jnp.where(kind > 0.5, wet_ref[1], value)
        value = jnp.where(kind > 1.5, wet_ref[2], value)
        value = jnp.where(kind > 2.5, wet_ref[3], value)
        return 1.0 + value

    level = level_of(widen(k0_ref[...], k1_ref[...]))
    sub16 = lax.broadcasted_iota(i32, (TILE, LANES), 0) < 4
    kind_halo = jnp.where(sub16, kb0_ref[...], kt0_ref[...])
    kind_halo1 = jnp.where(sub16, kb1_ref[...], kt1_ref[...])
    level_halo = level_of(widen(kind_halo, kind_halo1))
    depth = (lane_of() % CZ).astype(f32)
    up_gy, down_gy = ((gy + 7) % 8, (gy + 1) % 8)
    lane = lane_of()
    for s in range(2):
        tall = widen(h0_ref[s], h1_ref[s])
        for c in range(4):
            for by in range(BYD):
                act = act_tile(gy, by, c)
                for rr in range(4):
                    g = 4 * by + rr
                    height = tall[TILE * g : TILE * (g + 1), LANES * c : LANES * (c + 1)]
                    here = level[TILE * g : TILE * (g + 1), LANES * c : LANES * (c + 1)]
                    gas_ref[s, g, c] = jnp.where(depth < height * act, 0.0, here)
        halo = widen(
            jnp.where(sub16, hb0_ref[s], ht0_ref[s]), jnp.where(sub16, hb1_ref[s], ht1_ref[s])
        )
        for c in range(4):
            act = jnp.where(sub16, act_tile(down_gy, 0, c), act_tile(up_gy, 1, c))
            height = halo[:, LANES * c : LANES * (c + 1)]
            here = level_halo[:, LANES * c : LANES * (c + 1)]
            gas_ref[s, GROUPS, c] = jnp.where(depth < height * act, 0.0, here)
    packed = gas_ref[0, 0, 3]
    for g in range(1, GROUPS):
        packed = jnp.where(lane >= 16 * g, pltpu.roll(gas_ref[0, g, 3], 16 * g, 1), packed)
    packed_ref[...] = packed

    def step(g, carry):
        rows = pl.ds(pl.multiple_of(TILE * g, TILE), TILE)
        for c in range(3):
            f = [pop_ref[i, rows, LANES * c : LANES * (c + 1)] for i in range(Q)]
            out = collide(f, gas_ref[0, g, c])
            for i in range(Q):
                post_ref[i, c, rows, :] = out[i]
        return carry

    lax.fori_loop(0, GROUPS, step, 0)


def own_part(pos, owner, wetting, populations, heights, wall_class):
    n_y = heights.shape[1] // TILE
    n_x = heights.shape[2] // LANES

    def first_tile(pos):
        return (pos[1] * (BXD * B)) // LANES

    def second_tile(pos):
        return (first_tile(pos) + 1) % n_x

    def rows_above(pos):
        return (pos[0] * GROUPS + n_y - 1) % n_y

    def rows_below(pos):
        return (pos[0] * GROUPS + GROUPS) % n_y

    h_specs, k_specs = ([], [])
    for count, row in (
        (ROWS, lambda pos: pos[0]),
        (TILE, rows_above),
        (TILE, rows_below),
    ):
        for col in (first_tile, second_tile):
            h_specs.append(
                pl.BlockSpec(
                    (2, count, LANES), lambda g, pos, row=row, col=col: (0, row(pos), col(pos))
                )
            )
            k_specs.append(
                pl.BlockSpec(
                    (count, LANES), lambda g, pos, row=row, col=col: (row(pos), col(pos))
                )
            )
    smem = pl.BlockSpec(memory_space=pltpu.SMEM)
    return pl.pallas_call(
        own_kernel,
        grid_spec=pltpu.PrefetchScalarGridSpec(
            num_scalar_prefetch=1,
            grid=(1,),
            in_specs=[smem, smem, pl.BlockSpec((Q, ROWS, 3 * LANES), lambda g, pos: (0, 0, 0))]
            + h_specs
            + k_specs,
            out_specs=[
                pl.BlockSpec((Q, 3, ROWS, LANES), lambda g, pos: (0, 0, 0, 0)),
                pl.BlockSpec((2, GROUPS + 1, 4, TILE, LANES), lambda g, pos: (0, 0, 0, 0, 0)),
                pl.BlockSpec((TILE, LANES), lambda g, pos: (0, 0)),
            ],
        ),
        out_shape=[
            jax.ShapeDtypeStruct((Q, 3, ROWS, LANES), f32),
            jax.ShapeDtypeStruct((2, GROUPS + 1, 4, TILE, LANES), f32),
            jax.ShapeDtypeStruct((TILE, LANES), f32),
        ],
        compiler_params=params(),
        cost_estimate=pl.CostEstimate(flops=8_000_000, bytes_accessed=5_000_000, transcendentals=0),
        name="own_cells",
    )(pos, owner, wetting, populations, *([heights] * 6), *([wall_class] * 6))


def steps_kernel(own_ref, gas_ref, packed_ref, below_ref, above_ref, right_ref, out_ref, one, two, halo, sem):
    copy = pltpu.make_async_copy(own_ref, one.at[:, 0:3, pl.ds(BASE, ROWS), :], sem)
    copy.start()
    lane = lane_of()
    sub_low = row_of() < 4

    def keep_halo(ref, c, out):
        for i in range(Q):
            ref[i, c, BASE + ROWS : BASE + ROWS + TILE, :] = out[i]
            ref[i, c, BASE - TILE : BASE, :] = out[i]

    out = collide([right_ref[i] for i in range(Q)], packed_ref[...])
    for i in range(Q):
        for g in range(GROUPS):
            tile = out[i] if g == 0 else pltpu.roll(out[i], LANES - 16 * g, 1)
            one[i, 3, BASE + TILE * g : BASE + TILE * (g + 1), :] = tile
    corner = []
    for i in range(Q):
        tile, g = (right_ref[Q + i // 8], i % 8)
        corner.append(tile if g == 0 else pltpu.roll(tile, LANES - 16 * g, 1))
    keep_halo(one, 3, collide(corner, gas_ref[0, GROUPS, 3]))
    halo[...] = jnp.ones(halo.shape, f32)
    for i in range(Q):
        for c in range(3):
            cols = slice(LANES * c, LANES * (c + 1))
            halo[i, c, 0:2, :] = below_ref[2 * i : 2 * i + 2, cols]
            halo[i, c, TILE - 2 : TILE, :] = above_ref[2 * i : 2 * i + 2, cols]

    def halo_step(c, carry):
        out = collide([halo[i, c] for i in range(Q)], gas_ref[0, GROUPS, c])
        keep_halo(one, c, out)
        return carry

    lax.fori_loop(0, 3, halo_step, 0)
    copy.wait()

    def second(g, carry):
        def load(i, c, dy):
            return one[i, c, pl.ds(TILE * g + (BASE - dy), TILE), :]

        for c in range(4):
            out = collide([pull(load, i, c, lane, 0) for i in range(Q)], gas_ref[1, g, c])
            for i in range(Q):
                two[i, c, pl.ds(pl.multiple_of(TILE * g + BASE, TILE), TILE), :] = out[i]
        return carry

    lax.fori_loop(0, GROUPS, second, 0)

    def load_edges(i, c, dy):
        low = BASE + ROWS - dy
        high = BASE - TILE - dy
        return jnp.where(sub_low, one[i, c, low : low + TILE, :], one[i, c, high : high + TILE, :])

    for c in range(4):
        keep_halo(
            two,
            c,
            collide([pull(load_edges, i, c, lane, 0) for i in range(Q)], gas_ref[1, GROUPS, c]),
        )

    for by in range(BYD):

        def last(rr, carry):
            g = 4 * by + rr

            def load(i, c, dy):
                return two[i, c, pl.ds(TILE * g + (BASE - dy), TILE), :]

            for c in range(3):
                j = BXD * by + c
                tail = pull(load, TAIL, c, lane, 8)
                for n, i in enumerate(SENT):
                    value = pull(load, i, c, lane, 8)
                    if i in CARRIERS:
                        back = 3 - CARRIERS.index(i)
                        value = jnp.where(lane % CZ == CZ - 1, pltpu.roll(tail, back, 1), value)
                    if n < NDEV:
                        out_ref[n, pl.ds(pl.multiple_of(B * j + TILE * rr, TILE), TILE), :] = value
                    else:
                        m = 8 * (n - NDEV) + 2 * rr
                        at = BLK * B + 4 * j
                        out_ref[m, at : at + 4, :] = value[0:4]
                        out_ref[m + 1, at : at + 4, :] = value[4:8]
            return carry

        lax.fori_loop(0, 4, last, 0)


def steps(own, gas, packed, below, above, right):
    vmem = pl.BlockSpec(memory_space=pltpu.VMEM)
    return pl.pallas_call(
        steps_kernel,
        in_specs=[pl.BlockSpec(memory_space=pl.ANY)] + [vmem] * 5,
        out_specs=vmem,
        out_shape=jax.ShapeDtypeStruct((NDEV, PIECE, LANES), f32),
        scratch_shapes=[
            pltpu.VMEM((Q, 4, PADDED, LANES), f32),
            pltpu.VMEM((Q, 4, PADDED, LANES), f32),
            pltpu.VMEM((Q, 3, TILE, LANES), f32),
            pltpu.SemaphoreType.DMA,
        ],
        compiler_params=params(),
        cost_estimate=pl.CostEstimate(flops=20_000_000, bytes_accessed=6_000_000, transcendentals=0),
        name="two_steps",
    )(own, gas, packed, below, above, right)


def sort_kernel(table_ref, in_ref, out_ref):
    lane = lane_of()
    sub_low = row_of() < 4

    def source(entry):
        block = jnp.maximum(entry, 0)
        s = block // BLK
        j = block - s * BLK
        first = (j == 0) | (j == BXD)
        before_s = jnp.where(first, jnp.where(s == 0, NDEV - 1, s - 1), s)
        before_j = jnp.where(first, j + BXD - 1, j - 1)
        return (s, j, before_s, before_j)

    def receiver(d, carry):
        halves = []
        for k in range(CAP):
            entry = table_ref[d * CAP + k]
            valid = entry >= 0
            s, j, ps, pj = source(entry)
            for t in range(4):
                now = in_ref[s, pl.ds(pl.multiple_of(B * j + TILE * t, TILE), TILE), :]
                before = in_ref[ps, pl.ds(pl.multiple_of(B * pj + TILE * t, TILE), TILE), :]
                tile = pltpu.roll(jnp.where(lane >= 120, before, now), 8, 1)
                out_ref[d, B * k + TILE * t : B * k + TILE * (t + 1), :] = jnp.where(valid, tile, 0.0)

            def half(s, j):
                pair = j // 2
                tile = in_ref[s, pl.ds(pl.multiple_of(BLK * B + TILE * pair, TILE), TILE), :]
                return jnp.where(j - 2 * pair == k % 2, tile, pltpu.roll(tile, 4, 0))

            tile = pltpu.roll(jnp.where(lane >= 120, half(ps, pj), half(s, j)), 8, 1)
            halves.append(jnp.where(valid, tile, 0.0))
        for pair in range(CAP // 2):
            at = CAP * B + TILE * pair
            out_ref[d, at : at + TILE, :] = jnp.where(sub_low, halves[2 * pair], halves[2 * pair + 1])
        return carry

    lax.fori_loop(0, NDEV, receiver, 0)


def sort_blocks(table, arrived):
    vmem = pl.BlockSpec(memory_space=pltpu.VMEM)
    return pl.pallas_call(
        sort_kernel,
        in_specs=[pl.BlockSpec(memory_space=pltpu.SMEM), vmem],
        out_specs=vmem,
        out_shape=jax.ShapeDtypeStruct((NDEV, SLOTS, LANES), f32),
        compiler_params=params(),
        name="sort_blocks",
    )(table, arrived)


def restore_kernel(taken_ref, in_ref, out_ref):
    lane = lane_of()
    sub_low = row_of() < 4
    top = lane % CZ == CZ - 1
    place = lane % CZ

    def slot(k, taken, t):
        rows = slice(B * k + TILE * t, B * k + TILE * (t + 1))
        planes = {m: in_ref[m, rows, :] for m in range(NDEV)}
        pair = CAP * B + TILE * (k // 2)
        for p in range(2):
            a = in_ref[8 * p + 2 * t, pair : pair + TILE, :]
            b = in_ref[8 * p + 2 * t + 1, pair : pair + TILE, :]
            if k % 2 == 0:
                b = pltpu.roll(b, 4, 0)
            else:
                a = pltpu.roll(a, 4, 0)
            planes[NDEV + p] = jnp.where(sub_low, a, b)
        at = slice(TILE * t, TILE * (t + 1))
        last = taken * jnp.float32(WEIGHTS[TAIL])
        parts = [pltpu.roll(planes[i], LANES - 3 + n, 1) for n, i in enumerate(CARRIERS)]
        tail = jnp.where(place == 0, parts[0], jnp.where(place == 1, parts[1], parts[2]))
        out_ref[0, k, TAIL, at, :] = jnp.where(top, last, tail)
        for n, i in enumerate(SENT):
            value = planes[n]
            if i in FIXED_TOP:
                value = jnp.where(top, taken * jnp.float32(WEIGHTS[i]), value)
            out_ref[0, k, i, at, :] = value

    for k in range(CAP):
        taken = (taken_ref[0] > k).astype(f32)
        for t in range(4):
            slot(k, taken, t)


def restore(taken, arrived):
    vmem = pl.BlockSpec(memory_space=pltpu.VMEM)
    return pl.pallas_call(
        restore_kernel,
        in_specs=[pl.BlockSpec(memory_space=pltpu.SMEM), vmem],
        out_specs=vmem,
        out_shape=jax.ShapeDtypeStruct((1, CAP, Q, B, LANES), f32),
        compiler_params=params(),
        name="restore",
    )(taken, arrived)


def tables(owner, gy, gx):
    flat = lax.dynamic_index_in_dim(owner, gy, 0, keepdims=False).reshape(-1)
    number = jnp.arange(NDEV * BLK)
    same = (flat[:, None] == flat[None, :]) & (number[None, :] < number[:, None])
    slot = jnp.sum(same.astype(i32), axis=1)
    target = jnp.where(flat >= 0, flat * CAP + slot, -1)
    hit = target[:, None] == jnp.arange(NDEV * CAP)[None, :]
    table = jnp.max(jnp.where(hit, number[:, None], -1), axis=0).astype(i32)
    taken = jnp.sum((flat == gx).astype(i32)).reshape(1)
    return (table, taken)


def local(populations, heights, wall_class, wetting, owner):
    gy = lax.axis_index("gy")
    gx = lax.axis_index("gx")
    n_gy = lax.axis_size("gy")
    pos = jnp.stack([gy, gx]).astype(i32)
    up, down = pack_rows(populations)
    below = lax.ppermute(up, "gy", [(i, (i - 1) % n_gy) for i in range(n_gy)])
    above = lax.ppermute(down, "gy", [(i, (i + 1) % n_gy) for i in range(n_gy)])
    message = pack_cols(populations, below, above)
    right = lax.ppermute(message, "gx", [(i, (i - 1) % NDEV) for i in range(NDEV)])
    own, gas, packed = own_part(pos, owner.reshape(-1), wetting, populations, heights, wall_class)
    table, taken = tables(owner, gy, gx)
    spread = steps(own, gas, packed, below, above, right)
    gathered = lax.all_to_all(spread, "gx", split_axis=0, concat_axis=0, tiled=True)
    chosen = sort_blocks(table, gathered)
    arrived = lax.all_to_all(chosen, "gx", split_axis=0, concat_axis=0, tiled=True)
    return restore(taken, arrived)


def solution(mesh):
    return jax.shard_map(
        local,
        mesh=mesh,
        in_specs=(P(None, "gy", "gx"), P(), P(), P(), P()),
        out_specs=P("gy", "gx", None, None, None),
        check_vma=False,
    )
```

profile of v0, /device:TPU:6, one launch (start us, length us, event | category | flops | bytes accessed | tf_op | source)
XLA Modules:
  0.0 82.6 jit_solution(10586824691167955864)
XLA Ops:
  0.0 0.0 copy-start.2
  0.0 1.5 %copy-done.2 = f32[19,64,384]{2,1,0:T(8,128)S(1)} copy-done((f32[19,64,384]{2,1,0:T(8,128)S(1)}, f32[19,64,384]{2,1,0:T(8,128)}, u32[]{:S(2)}) %copy-start.2) | copy-done | bytes 1867800
  1.5 0.0 copy-start.6
  1.5 0.0 copy-start.1
  1.5 0.1 pack_rows.1
  1.6 0.0 copy-start.5
  1.6 0.3 collective-permute-start
  1.9 0.2 collective-permute-start.1
  2.1 0.1 copy-done.6
  2.2 0.1 copy.10
  2.4 0.1 reshape.29.owner_ref
  2.5 1.2 %collective-permute-done.below_ref = f32[40,384]{1,0:T(8,128)S(1)} collective-permute-done((f32[40,384]{1,0:T(8,128)S(1)}, f32[40,384]{1,0:T(8,128)S(1)}, u32[]{:S(2)}, u32[]{:S(2)}) %collective-permute-start) | collective-permute-done | bytes 61472 | tf_op jit(solution)/shard_map/ppermute | solution.py:574
  3.8 1.8 %collective-permute-done.1.above_ref = f32[40,384]{1,0:T(8,128)S(1)} collective-permute-done((f32[40,384]{1,0:T(8,128)S(1)}, f32[40,384]{1,0:T(8,128)S(1)}, u32[]{:S(2)}, u32[]{:S(2)}) %collective-permute-start.1) | collective-permute-done | bytes 61472 | tf_op jit(solution)/shard_map/ppermute | solution.py:575
  5.5 0.0 copy-start.3
  5.5 1.5 %copy-done.3 = f32[19,64,384]{2,1,0:T(8,128)S(1)} copy-done((f32[19,64,384]{2,1,0:T(8,128)S(1)}, f32[19,64,384]{2,1,0:T(8,128)}, u32[]{:S(2)}) %copy-start.3) | copy-done | bytes 1867800
  7.0 0.0 copy-start.4
  7.0 0.2 pack_cols.1
  7.3 6.6 %collective-permute-start.2 = (f32[22,8,128]{2,1,0:T(8,128)S(1)}, f32[22,8,128]{2,1,0:T(8,128)S(1)}, u32[]{:S(2)}, u32[]{:S(2)}) collective-permute-start(f32[22,8,128]{2,1,0:T(8,128)S(1)} %pack_cols.1), channel_id=1, source_target_pairs={{0,120},{8,0},{16,8},{24,16},{32,24},{40,32},{48,40},{56,48},{64,5... | collective-permute-start | bytes 270344 | tf_op jit(solution)/shard_map/ppermute | solution.py:577
  13.8 0.1 pad_add_fusion.pos_ref
  13.9 0.0 copy-done.1
  13.9 0.0 copy-done.5
  13.9 0.0 copy-done.4
  13.9 0.0 copy-start
  13.9 2.8 %copy-done = s32[2,512,1536]{2,1,0:T(8,128)S(1)} copy-done((s32[2,512,1536]{2,1,0:T(8,128)S(1)}, s32[2,512,1536]{2,1,0:T(8,128)}, u32[]{:S(2)}) %copy-start) | copy-done | bytes 6291480
  16.7 2.2 %own_cells.1 = (f32[19,3,64,128]{3,2,1,0:T(8,128)S(1)}, f32[2,9,4,8,128]{4,3,2,1,0:T(8,128)S(1)}, f32[8,128]{1,0:T(8,128)S(1)}) custom-call(s32[2]{0:T(128)S(1)} %pad_add_fusion.pos_ref, s32[768]{0:T(1024)S(1)} %reshape.29.owner_ref, f32[4]{0:T(128)S(1)} %copy-done.5, f32[19,64,384]{2,1,0:T(8,128)S(1)} %copy-done.4, s32[2,512,1536]{2,1,0:T(8,128)S(1)} %copy-done, ...), custom_call_target="tpu_custom_call" | custom-call | flops 8000000 | bytes 5000000 | tf_op jit(solution)/shard_map/own_cells/pallas_call | solution.py:325
  18.9 0.0 collective-permute-done.2.right_ref
  18.9 5.1 %two_steps.1 = f32[16,216,128]{2,1,0:T(8,128)} custom-call(f32[19,3,64,128]{3,2,1,0:T(8,128)S(1)} %get-tuple-element.10.own_ref, f32[2,9,4,8,128]{4,3,2,1,0:T(8,128)S(1)} %get-tuple-element.11.gas_ref, f32[8,128]{1,0:T(8,128)S(1)} %get-tuple-element.12.packed_ref, f32[40,384]{1,0:T(8,128)S(1)} %collective-permute-done.below_ref, ...), custom_call_target="tpu_custom_call" | custom-call | flops 20000000 | bytes 6000000 | tf_op jit(solution)/shard_map/two_steps/pallas_call | solution.py:440
  24.1 4.9 %all-to-all-start = ((f32[16,216,128]{2,1,0:T(8,128)}), f32[16,216,128]{2,1,0:T(8,128)S(1)}, u32[]{:S(2)}, u32[]{:S(2)}) async-start(f32[16,216,128]{2,1,0:T(8,128)} %two_steps.1), calls=%async_computation | async-start | bytes 3538944 | tf_op jit(solution)/shard_map/all_to_all | solution.py:581
  29.0 0.7 fusion.1
  29.7 0.1 copy.9
  29.8 0.1 reshape.28
  29.9 0.2 convert_reduce_fusion
  30.1 0.1 select_reduce_fusion.table_ref
  30.2 26.1 %all-to-all-done.in_ref = f32[16,216,128]{2,1,0:T(8,128)S(1)} async-done(((f32[16,216,128]{2,1,0:T(8,128)}), f32[16,216,128]{2,1,0:T(8,128)S(1)}, u32[]{:S(2)}, u32[]{:S(2)}) %all-to-all-start) | async-done | bytes 1769504 | tf_op jit(solution)/shard_map/all_to_all | solution.py:581
  56.2 3.0 %sort_blocks.1 = f32[16,144,128]{2,1,0:T(8,128)S(1)} custom-call(s32[64]{0:T(128)S(1)} %select_reduce_fusion.table_ref, f32[16,216,128]{2,1,0:T(8,128)S(1)} %all-to-all-done.in_ref), custom_call_target="tpu_custom_call" | custom-call | tf_op jit(solution)/shard_map/sort_blocks/pallas_call | solution.py:499
  59.2 21.6 %all_to_all.10.in_ref = f32[16,144,128]{2,1,0:T(8,128)S(1)} all-to-all(f32[16,144,128]{2,1,0:T(8,128)S(1)} %sort_blocks.1), channel_id=1, replica_groups=mesh['gx'=16,'gy'=8] {'gx'}, dimensions={0} | all-to-all | bytes 2359296 | tf_op jit(solution)/shard_map/all_to_all | solution.py:583
  80.8 1.8 %restore.1 = f32[1,4,19,32,128]{4,3,2,1,0:T(8,128)} custom-call(s32[1]{0:T(128)} %bitcast.taken_ref, f32[16,144,128]{2,1,0:T(8,128)S(1)} %all_to_all.10.in_ref), custom_call_target="tpu_custom_call" | custom-call | tf_op jit(solution)/shard_map/restore/pallas_call | solution.py:546
  (1 shorter events, 0.0 us)
Async XLA Ops:
  0.0 1.5 %copy-start.2 = (f32[19,64,384]{2,1,0:T(8,128)S(1)}, f32[19,64,384]{2,1,0:T(8,128)}, u32[]{:S(2)}) copy-start(f32[19,64,384]{2,1,0:T(8,128)} %pop_ref.3) | copy-start | bytes 5603332
  1.5 0.7 copy-start.6
  1.5 12.4 %copy-start.1 = (s32[512,1536]{1,0:T(8,128)S(1)}, s32[512,1536]{1,0:T(8,128)}, u32[]{:S(2)}) copy-start(s32[512,1536]{1,0:T(8,128)} %kb1_ref.1) | copy-start | bytes 9437188
  1.6 12.3 %copy-start.5 = (f32[4]{0:T(128)S(1)}, f32[4]{0:T(128)}, u32[]{:S(2)}) copy-start(f32[4]{0:T(128)} %wet_ref.1) | copy-start | bytes 52
  1.6 2.1 %collective-permute-start = (f32[40,384]{1,0:T(8,128)S(1)}, f32[40,384]{1,0:T(8,128)S(1)}, u32[]{:S(2)}, u32[]{:S(2)}) collective-permute-start(f32[40,384]{1,0:T(8,128)S(1)} %get-tuple-element.13), channel_id=1, source_target_pairs={{0,7},{1,0},{2,1},{3,2},{4,3},{5,4},{6,5},{7,6},{8,15},{9,8},{10,9... | collective-permute-start | bytes 184328 | tf_op jit(solution)/shard_map/ppermute | solution.py:574
  1.9 3.6 %collective-permute-start.1 = (f32[40,384]{1,0:T(8,128)S(1)}, f32[40,384]{1,0:T(8,128)S(1)}, u32[]{:S(2)}, u32[]{:S(2)}) collective-permute-start(f32[40,384]{1,0:T(8,128)S(1)} %get-tuple-element.14), channel_id=1, source_target_pairs={{0,1},{1,2},{2,3},{3,4},{4,5},{5,6},{6,7},{7,0},{8,9},{9,10},{10,1... | collective-permute-start | bytes 184328 | tf_op jit(solution)/shard_map/ppermute | solution.py:575
  5.5 1.5 %copy-start.3 = (f32[19,64,384]{2,1,0:T(8,128)S(1)}, f32[19,64,384]{2,1,0:T(8,128)}, u32[]{:S(2)}) copy-start(f32[19,64,384]{2,1,0:T(8,128)} %pop_ref.3) | copy-start | bytes 5603332
  7.0 6.9 %copy-start.4 = (f32[19,64,384]{2,1,0:T(8,128)S(1)}, f32[19,64,384]{2,1,0:T(8,128)}, u32[]{:S(2)}) copy-start(f32[19,64,384]{2,1,0:T(8,128)} %pop_ref.3) | copy-start | bytes 5603332
  7.3 11.6 %collective-permute-start.2 = (f32[22,8,128]{2,1,0:T(8,128)S(1)}, f32[22,8,128]{2,1,0:T(8,128)S(1)}, u32[]{:S(2)}, u32[]{:S(2)}) collective-permute-start(f32[22,8,128]{2,1,0:T(8,128)S(1)} %pack_cols.1), channel_id=1, source_target_pairs={{0,120},{8,0},{16,8},{24,16},{32,24},{40,32},{48,40},{56,48},{64,5... | collective-permute-start | bytes 270344 | tf_op jit(solution)/shard_map/ppermute | solution.py:577
  13.9 2.8 %copy-start = (s32[2,512,1536]{2,1,0:T(8,128)S(1)}, s32[2,512,1536]{2,1,0:T(8,128)}, u32[]{:S(2)}) copy-start(s32[2,512,1536]{2,1,0:T(8,128)} %hb1_ref.1) | copy-start | bytes 18874372
  24.1 32.2 %all-to-all-start = ((f32[16,216,128]{2,1,0:T(8,128)}), f32[16,216,128]{2,1,0:T(8,128)S(1)}, u32[]{:S(2)}, u32[]{:S(2)}) async-start(f32[16,216,128]{2,1,0:T(8,128)} %two_steps.1), calls=%async_computation | async-start | bytes 3538944 | tf_op jit(solution)/shard_map/all_to_all | solution.py:581
where the time goes:
time: 82.9 us; the launch traced here: 82.6 us
  waiting for transfers between devices  29.1 us (35%)
  blocking collectives  21.6 us (26%)
  Pallas kernels  12.4 us (15%)
  starting transfers between devices  12 us (14%)
  local copies, waits for them, and re-layouts  6.36 us (8%)
  other arithmetic  1.08 us (1%)
    all_to_all x1, waiting for transfers between devices, local(): lax.all_to_all(spread, 'gx', split_axis=0, concat_axis=0, tiled=True)  26.1 us
    all_to_all x1, blocking collectives, local(): lax.all_to_all(chosen, 'gx', split_axis=0, concat_axis=0, tiled=True)  21.6 us
    ppermute x1, starting transfers between devices, local(): lax.ppermute(message, 'gx', [(i, (i - 1) % NDEV) for i in range(NDEV)])  6.56 us
    unnamed x15, local copies, waits for them, and re-layouts  6.06 us
    pallas_call x1, Pallas kernels, steps(): pl.pallas_call(steps_kernel, in_specs=[pl.BlockSpec(memory_space=pl.ANY)]...  5.13 us
    all_to_all x1, starting transfers between devices, local(): lax.all_to_all(spread, 'gx', split_axis=0, concat_axis=0, tiled=True)  4.92 us
    pallas_call x1, Pallas kernels, sort_blocks(): pl.pallas_call(sort_kernel, in_specs=[pl.BlockSpec(memory_space=pltpu.SME...  2.97 us
    pallas_call x1, Pallas kernels, own_part(): pl.pallas_call(own_kernel, grid_spec=pltpu.PrefetchScalarGridSpec(num_sca...  2.21 us
  transfers between devices with their start and end apart: 4, of which 3 were waited for; matrix products, arithmetic and copies ran while one was open for 2% of the time, Pallas kernels for 3%

commit v1 on v0

v1 whole, which is shorter than its diff:
```python
import functools

import jax
import jax.numpy as jnp
import numpy as np
from jax import lax
from jax.experimental import pallas as pl
from jax.experimental.pallas import tpu as pltpu
from jax.sharding import PartitionSpec as P

B = 32
CZ = 4
BXD = 3
BYD = 2
CAP = 4
NCLS = 4
BLK = BXD * BYD
Q = 19
TILE = 8
LANES = 128
ROWS = 64
GROUPS = ROWS // TILE
SENT = [i for i in range(Q) if i != 17]
TAIL = 17
NDEV = 16
PIECE = BLK * (B + 4)
SLOTS = CAP * (B + 4)

VELOCITY = [
    (0, 0, 0),
    (1, 0, 0),
    (-1, 0, 0),
    (0, 1, 0),
    (0, -1, 0),
    (0, 0, 1),
    (0, 0, -1),
    (1, 1, 0),
    (-1, -1, 0),
    (1, -1, 0),
    (-1, 1, 0),
    (1, 0, 1),
    (-1, 0, -1),
    (1, 0, -1),
    (-1, 0, 1),
    (0, 1, 1),
    (0, -1, -1),
    (0, 1, -1),
    (0, -1, 1),
]
WEIGHTS = [1.0 / 3.0] + [1.0 / 18.0] * 6 + [1.0 / 36.0] * 12
OPPOSITE = [0, 2, 1, 4, 3, 6, 5, 8, 7, 10, 9, 12, 11, 14, 13, 16, 15, 18, 17]
CARRIERS = (6, 12, 13)
FIXED_TOP = (6, 12, 13, 16)

f32 = jnp.float32
i32 = jnp.int32
MIB = 1024 * 1024


def params(limit=16 * MIB):
    return pltpu.CompilerParams(vmem_limit_bytes=limit)


VMEM_SPEC = pl.BlockSpec(memory_space=pltpu.VMEM)
HBM_SPEC = pl.BlockSpec(memory_space=pltpu.HBM)
SMEM_SPEC = pl.BlockSpec(memory_space=pltpu.SMEM)
OWN_SHAPE = jax.ShapeDtypeStruct((Q, 3, ROWS, LANES), f32)
TWO_SHAPE = jax.ShapeDtypeStruct((Q, 4, ROWS, LANES), f32)
RIGHT_SHAPE = jax.ShapeDtypeStruct((Q, ROWS, LANES), f32)
EDGE_SHAPE = jax.ShapeDtypeStruct((2 * Q + 2, 4 * LANES), f32)
MESSAGE_SHAPE = jax.ShapeDtypeStruct((NDEV, PIECE, LANES), f32)
HALVES_SHAPE = jax.ShapeDtypeStruct((NDEV, 4 * BLK, LANES), f32)


def lane_of():
    return lax.broadcasted_iota(i32, (TILE, LANES), 1)


def row_of():
    return lax.broadcasted_iota(i32, (TILE, LANES), 0)


def collide(f, gas):
    pairs = [(i, i + 1) for i in range(1, Q, 2)]
    total = {i: f[i] + f[o] for i, o in pairs}
    diff = {i: f[i] - f[o] for i, o in pairs}
    rho = f[0]
    for i, _ in pairs:
        rho = rho + total[i]
    jx = diff[1] + diff[7] + diff[9] + diff[11] + diff[13]
    jy = diff[3] + diff[7] - diff[9] + diff[15] + diff[17]
    jz = diff[5] + diff[11] - diff[13] + diff[15] - diff[17]
    inv = 1.0 / rho
    scaled = rho - 1.5 * inv * (jx * jx + jy * jy + jz * jz)
    along = {
        1: jx,
        3: jy,
        5: jz,
        7: jx + jy,
        9: jx - jy,
        11: jx + jz,
        13: jx - jz,
        15: jy + jz,
        17: jy - jz,
    }
    is_gas = gas > 0
    out = [None] * Q
    out[0] = jnp.where(
        is_gas, WEIGHTS[0] * gas, -0.6 * f[0] + (1.6 * WEIGHTS[0]) * scaled
    )
    for first, last in ((1, 5), (7, 17)):
        w = WEIGHTS[first]
        base = (1.6 * w) * scaled
        bend = (7.2 * w) * inv
        held = w * gas
        for i in range(first, last + 1, 2):
            cj = along[i]
            even = base + bend * (cj * cj) - 0.3 * total[i]
            odd = 0.25 * diff[i] + (1.5 * w) * cj
            out[i] = jnp.where(is_gas, held, even + odd)
            out[i + 1] = jnp.where(is_gas, held, even - odd)
    return out


def shifted(load, c, shift, lane):
    if shift == 0:
        return load(c)
    if shift > 0:
        here = load(c)
        if c > 0:
            here = jnp.where(lane >= LANES - shift, load(c - 1), here)
        return pltpu.roll(here, shift, 1)
    here = load(c)
    if c < 3:
        here = jnp.where(lane < -shift, load(c + 1), here)
    return pltpu.roll(here, LANES + shift, 1)


def pull(load, i, c, lane, extra):
    cx, cy, cz = VELOCITY[i]
    moved = shifted(lambda t: load(i, t, cy), c, 4 * cx + cz - extra, lane)
    if cz == 1:
        wall = shifted(lambda t: load(OPPOSITE[i], t, 0), c, -extra, lane)
        moved = jnp.where(lane % CZ == 0, wall, moved)
    elif cz == -1:
        moved = jnp.where(lane % CZ == CZ - 1, jnp.float32(WEIGHTS[i]), moved)
    return moved


def pack_cols_kernel(pop_ref, out_ref, buf, sem):
    copies = []
    for g in range(GROUPS):
        rows = pl.ds(TILE * g, TILE)
        copies.append(
            pltpu.make_async_copy(
                pop_ref.at[:, rows, pl.ds(0, LANES)], buf.at[:, rows, :], sem.at[g]
            )
        )
        copies[-1].start()
    for copy in copies:
        copy.wait()
    lane = lane_of()
    for i in range(Q):
        packed = buf[i, 0:TILE, :]
        for g in range(1, GROUPS):
            rolled = pltpu.roll(buf[i, TILE * g : TILE * (g + 1), :], 16 * g, 1)
            packed = jnp.where(lane >= 16 * g, rolled, packed)
        out_ref[i] = packed


def pack_cols(populations):
    return pl.pallas_call(
        pack_cols_kernel,
        in_specs=[HBM_SPEC],
        out_specs=VMEM_SPEC,
        out_shape=jax.ShapeDtypeStruct((Q, TILE, LANES), f32),
        scratch_shapes=[pltpu.VMEM((Q, ROWS, LANES), f32), pltpu.SemaphoreType.DMA((GROUPS,))],
        compiler_params=params(63 * MIB),
        name="pack_cols",
    )(populations)


def own_kernel(
    owner_ref,
    wet_ref,
    pop_hbm,
    height_hbm,
    kind_hbm,
    post_ref,
    gas_ref,
    packed_ref,
    up_ref,
    down_ref,
    pop,
    height,
    kind,
    pop_sem,
    field_sem,
):
    gy, gx = (lax.axis_index("gy"), lax.axis_index("gx"))
    n_gy = height_hbm.shape[1] // ROWS
    n_x = height_hbm.shape[2] // LANES
    first = (gx * (BXD * B)) // LANES
    offset = gx * (BXD * B) - first * LANES
    second = lax.rem(first + 1, n_x)
    up_gy, down_gy = (lax.rem(gy + n_gy - 1, n_gy), lax.rem(gy + 1, n_gy))
    copies = []
    for half, col in enumerate((first, second)):
        cols = pl.ds(pl.multiple_of(col * LANES, LANES), LANES)
        to = pl.ds(LANES * half, LANES)
        for row, at, count in (
            (gy * ROWS, TILE, ROWS),
            (up_gy * ROWS + ROWS - TILE, 0, TILE),
            (down_gy * ROWS, TILE + ROWS, TILE),
        ):
            rows = pl.ds(pl.multiple_of(row, TILE), count)
            n = len(copies)
            copies.append(
                pltpu.make_async_copy(
                    height_hbm.at[:, rows, cols], height.at[:, pl.ds(at, count), to], field_sem.at[n]
                )
            )
            copies.append(
                pltpu.make_async_copy(
                    kind_hbm.at[rows, cols], kind.at[pl.ds(at, count), to], field_sem.at[n + 1]
                )
            )
    for copy in copies:
        copy.start()

    def pop_copy(g):
        rows = pl.ds(pl.multiple_of(TILE * g, TILE), TILE)
        return pltpu.make_async_copy(pop_hbm.at[:, rows, :], pop.at[:, rows, :], pop_sem.at[g])

    for g in range(GROUPS):
        pop_copy(g).start()

    wide = 4 * LANES
    cell = lax.broadcasted_iota(i32, (2 * LANES, wide), 0)
    place = lax.broadcasted_iota(i32, (2 * LANES, wide), 1)
    spread = (cell == offset + place // CZ).astype(f32)

    def widen(values):
        return jnp.dot(values.astype(f32), spread, preferred_element_type=f32)

    def active(row, col, j):
        return (owner_ref[j, row, col] >= 0).astype(f32)

    next_gx = lax.rem(gx + 1, NDEV)

    def act_tile(row, by, c):
        return active(row, gx, BXD * by + c) if c < BXD else active(row, next_gx, BXD * by)

    for copy in copies:
        copy.wait()
    kinds = widen(kind[...])
    value = wet_ref[0]
    for n in range(1, NCLS):
        value = jnp.where(kinds > n - 0.5, wet_ref[n], value)
    level = 1.0 + value
    lane = lane_of()
    depth = (lane % CZ).astype(f32)
    sub_low = row_of() < 4
    low, high = (TILE + ROWS, 0)
    for s in range(2):
        tall = widen(height[s])
        for c in range(4):
            cols = slice(LANES * c, LANES * (c + 1))
            for by in range(BYD):
                act = act_tile(gy, by, c)
                for rr in range(4):
                    g = 4 * by + rr
                    rows = slice(TILE * (g + 1), TILE * (g + 2))
                    fluid = depth < tall[rows, cols] * act
                    gas_ref[s, g, c] = jnp.where(fluid, 0.0, level[rows, cols])
            act = jnp.where(sub_low, act_tile(down_gy, 0, c), act_tile(up_gy, 1, c))
            here = jnp.where(sub_low, tall[low : low + TILE, cols], tall[high : high + TILE, cols])
            wall = jnp.where(sub_low, level[low : low + TILE, cols], level[high : high + TILE, cols])
            gas_ref[s, GROUPS, c] = jnp.where(depth < here * act, 0.0, wall)
    packed = gas_ref[0, 0, 3]
    for g in range(1, GROUPS):
        packed = jnp.where(lane >= 16 * g, pltpu.roll(gas_ref[0, g, 3], 16 * g, 1), packed)
    packed_ref[...] = packed

    def step(g, carry):
        pop_copy(g).wait()
        rows = pl.ds(pl.multiple_of(TILE * g, TILE), TILE)
        for c in range(3):
            f = [pop[i, rows, LANES * c : LANES * (c + 1)] for i in range(Q)]
            out = collide(f, gas_ref[0, g, c])
            for i in range(Q):
                post_ref[i, c, rows, :] = out[i]
        return carry

    lax.fori_loop(0, GROUPS, step, 0)
    for i in range(Q):
        up_ref[2 * i : 2 * i + 2, :] = pop[i, 0:2, :]
        down_ref[2 * i : 2 * i + 2, :] = pop[i, ROWS - 2 : ROWS, :]


def own_part(owner, wetting, populations, heights, wall_class):
    return pl.pallas_call(
        own_kernel,
        in_specs=[SMEM_SPEC, SMEM_SPEC, HBM_SPEC, HBM_SPEC, HBM_SPEC],
        out_specs=[VMEM_SPEC] * 5,
        out_shape=[
            OWN_SHAPE,
            jax.ShapeDtypeStruct((2, GROUPS + 1, 4, TILE, LANES), f32),
            jax.ShapeDtypeStruct((TILE, LANES), f32),
            jax.ShapeDtypeStruct((2 * Q + 2, 3 * LANES), f32),
            jax.ShapeDtypeStruct((2 * Q + 2, 3 * LANES), f32),
        ],
        scratch_shapes=[
            pltpu.VMEM((Q, ROWS, 3 * LANES), f32),
            pltpu.VMEM((2, ROWS + 2 * TILE, 2 * LANES), i32),
            pltpu.VMEM((ROWS + 2 * TILE, 2 * LANES), i32),
            pltpu.SemaphoreType.DMA((GROUPS,)),
            pltpu.SemaphoreType.DMA((12,)),
        ],
        compiler_params=params(50 * MIB),
        cost_estimate=pl.CostEstimate(flops=8_000_000, bytes_accessed=8_000_000, transcendentals=0),
        name="own_cells",
    )(owner, wetting, populations, heights, wall_class)


def pack_rows_kernel(up_in, down_in, right_ref, up_ref, down_ref):
    up_ref[:, 0 : 3 * LANES] = up_in[...]
    down_ref[:, 0 : 3 * LANES] = down_in[...]
    for i in range(Q):
        up_ref[2 * i : 2 * i + 2, 3 * LANES :] = right_ref[i, 0:2, :]
        last = pltpu.roll(right_ref[i], 16, 1)
        down_ref[2 * i : 2 * i + 2, 3 * LANES :] = last[TILE - 2 : TILE]


def pack_rows(up, down, right):
    return pl.pallas_call(
        pack_rows_kernel,
        in_specs=[VMEM_SPEC] * 3,
        out_specs=[VMEM_SPEC] * 2,
        out_shape=[EDGE_SHAPE, EDGE_SHAPE],
        compiler_params=params(),
        name="pack_rows",
    )(up, down, right)


def store_running(load, out_ref, halves_ref, by, rr, lane):
    for c in range(3):
        j = BXD * by + c
        tail = pull(load, TAIL, c, lane, 8)
        for n, i in enumerate(SENT):
            value = pull(load, i, c, lane, 8)
            if i in CARRIERS:
                back = 3 - CARRIERS.index(i)
                value = jnp.where(lane % CZ == CZ - 1, pltpu.roll(tail, back, 1), value)
            if n < NDEV:
                out_ref[n, B * j + TILE * rr : B * j + TILE * (rr + 1), :] = value
            else:
                m = 8 * (n - NDEV) + 2 * rr
                halves_ref[m, 4 * j : 4 * j + 4, :] = value[0:4]
                halves_ref[m + 1, 4 * j : 4 * j + 4, :] = value[4:8]


INNER = ((0, 2), (0, 3), (1, 0), (1, 1))
OUTER = ((0, 0), (0, 1), (1, 2), (1, 3))


def message_copy(buf, out_hbm, sem, j, start):
    rows = pl.ds(B * j + start, 2 * TILE)
    return pltpu.make_async_copy(buf.at[:, rows, :], out_hbm.at[:, rows, :], sem.at[j])


def inner_kernel(own_ref, gas_ref, packed_ref, right_ref, post_ref, two_ref, halves_ref, out_hbm, buf, sem):
    lane = lane_of()
    out = collide([right_ref[i] for i in range(Q)], packed_ref[...])
    for i in range(Q):
        for g in range(GROUPS):
            tile = out[i] if g == 0 else pltpu.roll(out[i], LANES - 16 * g, 1)
            post_ref[i, TILE * g : TILE * (g + 1), :] = tile

    def second(g, carry):
        def load(i, c, dy):
            rows = pl.ds(TILE * g - dy, TILE)
            return own_ref[i, c, rows, :] if c < 3 else post_ref[i, rows, :]

        for c in range(4):
            out = collide([pull(load, i, c, lane, 0) for i in range(Q)], gas_ref[1, g, c])
            for i in range(Q):
                two_ref[i, c, pl.ds(pl.multiple_of(TILE * g, TILE), TILE), :] = out[i]
        return carry

    lax.fori_loop(1, GROUPS - 1, second, 0)
    copies = []
    for by, rr in INNER:
        at = TILE * (4 * by + rr)
        store_running(
            lambda i, c, dy: two_ref[i, c, at - dy : at - dy + TILE, :], buf, halves_ref, by, rr, lane
        )
        if rr % 2 == 1:
            for c in range(3):
                copies.append(message_copy(buf, out_hbm, sem, BXD * by + c, TILE * (rr - 1)))
                copies[-1].start()
    for copy in copies:
        copy.wait()


def inner_part(own, gas, packed, right):
    return pl.pallas_call(
        inner_kernel,
        in_specs=[VMEM_SPEC] * 4,
        out_specs=[VMEM_SPEC, VMEM_SPEC, VMEM_SPEC, HBM_SPEC],
        out_shape=[RIGHT_SHAPE, TWO_SHAPE, HALVES_SHAPE, MESSAGE_SHAPE],
        scratch_shapes=[pltpu.VMEM((NDEV, BLK * B, LANES), f32), pltpu.SemaphoreType.DMA((BLK,))],
        compiler_params=params(),
        cost_estimate=pl.CostEstimate(flops=8_000_000, bytes_accessed=8_000_000, transcendentals=0),
        name="inner_rows",
    )(own, gas, packed, right)


def edge_kernel(
    message_in,
    halves_in,
    own_ref,
    post_ref,
    two_ref,
    gas_ref,
    below_ref,
    above_ref,
    out_hbm,
    halo,
    top,
    bottom,
    top_two,
    bottom_two,
    buf,
    halves,
    sem,
    half_sem,
):
    lane = lane_of()
    sub_low = row_of() < 4
    tall = ROWS - TILE

    halves[...] = halves_in[...]
    halo[...] = jnp.ones(halo.shape, f32)
    for i in range(Q):
        for c in range(4):
            cols = slice(LANES * c, LANES * (c + 1))
            halo[i, c, 0:2, :] = below_ref[2 * i : 2 * i + 2, cols]
            halo[i, c, TILE - 2 : TILE, :] = above_ref[2 * i : 2 * i + 2, cols]
            first = own_ref[i, c, 0:TILE, :] if c < 3 else post_ref[i, 0:TILE, :]
            last = own_ref[i, c, tall:ROWS, :] if c < 3 else post_ref[i, tall:ROWS, :]
            top[i, c, 16:24, :] = first
            bottom[i, c, 8:16, :] = last
            top_two[i, c, 24:32, :] = two_ref[i, c, TILE : 2 * TILE, :]
            bottom_two[i, c, 8:16, :] = two_ref[i, c, tall - TILE : tall, :]
    for c in range(4):
        out = collide([halo[i, c] for i in range(Q)], gas_ref[0, GROUPS, c])
        for i in range(Q):
            top[i, c, 8:16, :] = out[i]
            bottom[i, c, 16:24, :] = out[i]

    def load_first(i, c, dy):
        if dy == 1:
            return top[i, c, 15:23, :]
        return own_ref[i, c, -dy : TILE - dy, :] if c < 3 else post_ref[i, -dy : TILE - dy, :]

    def load_last(i, c, dy):
        if dy == -1:
            return bottom[i, c, 9:17, :]
        return own_ref[i, c, tall - dy : ROWS - dy, :] if c < 3 else post_ref[i, tall - dy : ROWS - dy, :]

    def load_halo(i, c, dy):
        return jnp.where(sub_low, bottom[i, c, 16 - dy : 24 - dy, :], top[i, c, 8 - dy : 16 - dy, :])

    for c in range(4):
        out = collide([pull(load_first, i, c, lane, 0) for i in range(Q)], gas_ref[1, 0, c])
        for i in range(Q):
            top_two[i, c, 16:24, :] = out[i]
        out = collide([pull(load_last, i, c, lane, 0) for i in range(Q)], gas_ref[1, GROUPS - 1, c])
        for i in range(Q):
            bottom_two[i, c, 16:24, :] = out[i]
        out = collide([pull(load_halo, i, c, lane, 0) for i in range(Q)], gas_ref[1, GROUPS, c])
        for i in range(Q):
            top_two[i, c, 8:16, :] = out[i]
            bottom_two[i, c, 24:32, :] = out[i]

    copies = []
    for by, rr in OUTER:
        g = 4 * by + rr

        def load(i, c, dy):
            if by == 0 and (g == 0 or dy == 1):
                return top_two[i, c, 16 + TILE * g - dy : 24 + TILE * g - dy, :]
            if by == 1 and (g == GROUPS - 1 or dy == -1):
                at = TILE * (g - GROUPS + 3) - dy
                return bottom_two[i, c, at : at + TILE, :]
            return two_ref[i, c, TILE * g - dy : TILE * (g + 1) - dy, :]

        store_running(load, buf, halves, by, rr, lane)
        if rr % 2 == 1:
            for c in range(3):
                copies.append(message_copy(buf, out_hbm, sem, BXD * by + c, TILE * (rr - 1)))
                copies[-1].start()
    copies.append(
        pltpu.make_async_copy(halves, out_hbm.at[:, pl.ds(BLK * B, 4 * BLK), :], half_sem)
    )
    copies[-1].start()
    for copy in copies:
        copy.wait()


def edge_part(message, halves, own, post, two, gas, below, above):
    return pl.pallas_call(
        edge_kernel,
        in_specs=[HBM_SPEC] + [VMEM_SPEC] * 7,
        out_specs=HBM_SPEC,
        out_shape=MESSAGE_SHAPE,
        input_output_aliases={0: 0},
        scratch_shapes=[
            pltpu.VMEM((Q, 4, TILE, LANES), f32),
            pltpu.VMEM((Q, 4, 3 * TILE, LANES), f32),
            pltpu.VMEM((Q, 4, 4 * TILE, LANES), f32),
            pltpu.VMEM((Q, 4, 4 * TILE, LANES), f32),
            pltpu.VMEM((Q, 4, 4 * TILE, LANES), f32),
            pltpu.VMEM((NDEV, BLK * B, LANES), f32),
            pltpu.VMEM((NDEV, 4 * BLK, LANES), f32),
            pltpu.SemaphoreType.DMA((BLK,)),
            pltpu.SemaphoreType.DMA,
        ],
        compiler_params=params(),
        cost_estimate=pl.CostEstimate(flops=8_000_000, bytes_accessed=8_000_000, transcendentals=0),
        name="edge_rows",
    )(message, halves, own, post, two, gas, below, above)


def sort_kernel(table_ref, in_ref, out_ref):
    lane = lane_of()
    sub_low = row_of() < 4
    count = NDEV * CAP

    def receiver(d, carry):
        halves = []
        for k in range(CAP):
            n = d * CAP + k
            valid = table_ref[n] >= 0
            s, j = (table_ref[count + n], table_ref[2 * count + n])
            ps, pj = (table_ref[3 * count + n], table_ref[4 * count + n])
            for t in range(4):
                now = in_ref[s, pl.ds(pl.multiple_of(B * j + TILE * t, TILE), TILE), :]
                before = in_ref[ps, pl.ds(pl.multiple_of(B * pj + TILE * t, TILE), TILE), :]
                tile = pltpu.roll(jnp.where(lane >= 120, before, now), 8, 1)
                out_ref[d, B * k + TILE * t : B * k + TILE * (t + 1), :] = jnp.where(valid, tile, 0.0)

            def half(s, j):
                pair = lax.shift_right_logical(j, 1)
                tile = in_ref[s, pl.ds(pl.multiple_of(BLK * B + TILE * pair, TILE), TILE), :]
                return jnp.where(j - 2 * pair == k % 2, tile, pltpu.roll(tile, 4, 0))

            tile = pltpu.roll(jnp.where(lane >= 120, half(ps, pj), half(s, j)), 8, 1)
            halves.append(jnp.where(valid, tile, 0.0))
        for pair in range(CAP // 2):
            at = CAP * B + TILE * pair
            out_ref[d, at : at + TILE, :] = jnp.where(sub_low, halves[2 * pair], halves[2 * pair + 1])
        return carry

    lax.fori_loop(0, NDEV, receiver, 0, unroll=4)


def sort_blocks(table, arrived):
    return pl.pallas_call(
        sort_kernel,
        in_specs=[SMEM_SPEC, VMEM_SPEC],
        out_specs=VMEM_SPEC,
        out_shape=jax.ShapeDtypeStruct((NDEV, SLOTS, LANES), f32),
        compiler_params=params(),
        name="sort_blocks",
    )(table, arrived)


def restore_kernel(taken_ref, in_ref, out_hbm, buf, sem):
    lane = lane_of()
    sub_low = row_of() < 4
    top = lane % CZ == CZ - 1
    place = lane % CZ

    def slot(k, taken, t):
        rows = slice(B * k + TILE * t, B * k + TILE * (t + 1))
        planes = {m: in_ref[m, rows, :] for m in range(NDEV)}
        pair = CAP * B + TILE * (k // 2)
        for p in range(2):
            a = in_ref[8 * p + 2 * t, pair : pair + TILE, :]
            b = in_ref[8 * p + 2 * t + 1, pair : pair + TILE, :]
            if k % 2 == 0:
                b = pltpu.roll(b, 4, 0)
            else:
                a = pltpu.roll(a, 4, 0)
            planes[NDEV + p] = jnp.where(sub_low, a, b)
        at = slice(TILE * t, TILE * (t + 1))
        last = taken * jnp.float32(WEIGHTS[TAIL])
        parts = [pltpu.roll(planes[i], LANES - 3 + n, 1) for n, i in enumerate(CARRIERS)]
        tail = jnp.where(place == 0, parts[0], jnp.where(place == 1, parts[1], parts[2]))
        buf[k, TAIL, at, :] = jnp.where(top, last, tail)
        for n, i in enumerate(SENT):
            value = planes[n]
            if i in FIXED_TOP:
                value = jnp.where(top, taken * jnp.float32(WEIGHTS[i]), value)
            buf[k, i, at, :] = value

    copies = [pltpu.make_async_copy(buf.at[k], out_hbm.at[0, k], sem.at[k]) for k in range(CAP)]
    for k in range(CAP):
        taken = (taken_ref[0] > k).astype(f32)
        for t in range(4):
            slot(k, taken, t)
        copies[k].start()
    for copy in copies:
        copy.wait()


def restore(taken, arrived):
    return pl.pallas_call(
        restore_kernel,
        in_specs=[SMEM_SPEC, VMEM_SPEC],
        out_specs=HBM_SPEC,
        out_shape=jax.ShapeDtypeStruct((1, CAP, Q, B, LANES), f32),
        scratch_shapes=[pltpu.VMEM((CAP, Q, B, LANES), f32), pltpu.SemaphoreType.DMA((CAP,))],
        compiler_params=params(),
        name="restore",
    )(taken, arrived)


def tables(owner, gy, gx):
    flat = lax.dynamic_index_in_dim(owner, gy, 0, keepdims=False).reshape(-1)
    number = jnp.arange(NDEV * BLK)
    same = (flat[:, None] == flat[None, :]) & (number[None, :] < number[:, None])
    slot = jnp.sum(same.astype(i32), axis=1)
    target = jnp.where(flat >= 0, flat * CAP + slot, -1)
    hit = target[:, None] == jnp.arange(NDEV * CAP)[None, :]
    table = jnp.max(jnp.where(hit, number[:, None], -1), axis=0).astype(i32)
    block = jnp.maximum(table, 0)
    s, j = (block // BLK, block % BLK)
    at_edge = j % BXD == 0
    before_s = jnp.where(at_edge, (s + NDEV - 1) % NDEV, s)
    before_j = jnp.where(at_edge, j + BXD - 1, j - 1)
    taken = jnp.sum((flat == gx).astype(i32)).reshape(1)
    return (jnp.concatenate([table, s, j, before_s, before_j]), taken)


def local(populations, heights, wall_class, wetting, owner):
    gy = lax.axis_index("gy")
    gx = lax.axis_index("gx")
    n_gy = lax.axis_size("gy")
    right = lax.ppermute(pack_cols(populations), "gx", [(i, (i - 1) % NDEV) for i in range(NDEV)])
    own, gas, packed, up, down = own_part(
        owner.transpose(2, 0, 1), wetting, populations, heights, wall_class
    )
    up, down = pack_rows(up, down, right)
    below = lax.ppermute(up, "gy", [(i, (i - 1) % n_gy) for i in range(n_gy)])
    above = lax.ppermute(down, "gy", [(i, (i + 1) % n_gy) for i in range(n_gy)])
    post, two, halves, message = inner_part(own, gas, packed, right)
    message = edge_part(message, halves, own, post, two, gas, below, above)
    table, taken = tables(owner, gy, gx)
    gathered = lax.all_to_all(message, "gx", split_axis=0, concat_axis=0, tiled=True)
    chosen = sort_blocks(table, gathered)
    arrived = lax.all_to_all(chosen, "gx", split_axis=0, concat_axis=0, tiled=True)
    return restore(taken, arrived)


def solution(mesh):
    return jax.shard_map(
        local,
        mesh=mesh,
        in_specs=(P(None, "gy", "gx"), P(), P(), P(), P()),
        out_specs=P("gy", "gx", None, None, None),
        check_vma=False,
    )
```

time: 82.9 us -> 80.7 us (0.973)
  local copies, waits for them, and re-layouts: 6.36 us -> 0.26 us
  Pallas kernels: 12.4 us -> 14.9 us
    unnamed x15 -> x4, local copies, waits for them, and re-layouts: 6.06 us -> 0.01 us
    all_to_all x1, waiting for transfers between devices: 26.1 us -> 29.1 us  [local(): lax.all_to_all(message, 'gx', split_axis=0, concat_axis=0, tiled=True)]
    pallas_call x6 -> x7, Pallas kernels: 12.4 us -> 14.9 us  [the longest x1 3.62 us: own_part(): pl.pallas_call(own_kernel, in_specs=[SMEM_SPEC, SMEM_SPEC, HBM_SPEC, HBM_...]
    ppermute x1, waiting for transfers between devices: 1.78 us -> 0.08 us  [local(): above = lax.ppermute(down, 'gy', [(i, (i + 1) % n_gy) for i in range(n_gy)])]
    ppermute x1, waiting for transfers between devices: 1.24 us -> 0.01 us  [local(): below = lax.ppermute(up, 'gy', [(i, (i - 1) % n_gy) for i in range(n_gy)])]
  transfers between devices with their start and end apart: 4 -> 4, of which waited for: 3 -> 2; matrix products, arithmetic and copies ran while one was open for 2% -> 2% of each run, Pallas kernels for 3% -> 9%
where the time goes in v1:
time: 80.7 us; the launch traced here: 80.4 us
  waiting for transfers between devices  29.2 us (36%)
  blocking collectives  22.1 us (27%)
  Pallas kernels  14.9 us (18%)
  starting transfers between devices  12.7 us (16%)
  other arithmetic  1.07 us (1%)
    all_to_all x1, waiting for transfers between devices, local(): lax.all_to_all(message, 'gx', split_axis=0, concat_axis=0, tiled=True)  29.1 us
    all_to_all x1, blocking collectives, local(): lax.all_to_all(chosen, 'gx', split_axis=0, concat_axis=0, tiled=True)  22.1 us
    ppermute x1, starting transfers between devices, local(): lax.ppermute(pack_cols(populations), 'gx', [(i, (i - 1) % NDEV) for i in...  6.56 us
    all_to_all x1, starting transfers between devices, local(): lax.all_to_all(message, 'gx', split_axis=0, concat_axis=0, tiled=True)  5.68 us
    pallas_call x1, Pallas kernels, own_part(): pl.pallas_call(own_kernel, in_specs=[SMEM_SPEC, SMEM_SPEC, HBM_SPEC, HBM_...  3.62 us
    pallas_call x1, Pallas kernels, inner_part(): pl.pallas_call(inner_kernel, in_specs=[VMEM_SPEC] * 4, out_specs=[VMEM_SP...  3.28 us
    pallas_call x1, Pallas kernels, edge_part(): pl.pallas_call(edge_kernel, in_specs=[HBM_SPEC] + [VMEM_SPEC] * 7, out_sp...  2.49 us
    pallas_call x1, Pallas kernels, pack_cols(): pl.pallas_call(pack_cols_kernel, in_specs=[HBM_SPEC], out_specs=VMEM_SPEC...  2.08 us
  transfers between devices with their start and end apart: 4, of which 2 were waited for; matrix products, arithmetic and copies ran while one was open for 2% of the time, Pallas kernels for 9%

profile of v1, /device:TPU:6, one launch (start us, length us, event | category | flops | bytes accessed | tf_op | source)
XLA Modules:
  0.0 80.4 jit_solution(14723791392167721328)
XLA Ops:
  0.0 0.0 copy-start
  0.0 0.0 copy-start.1
  0.0 2.1 %pack_cols.1 = f32[19,8,128]{2,1,0:T(8,128)} custom-call(f32[19,64,384]{2,1,0:T(8,128)} %pop_ref.1), custom_call_target="tpu_custom_call" | custom-call | tf_op jit(solution)/shard_map/pack_cols/pallas_call | solution.py:172
  2.1 6.6 %collective-permute-start = (f32[19,8,128]{2,1,0:T(8,128)}, f32[19,8,128]{2,1,0:T(8,128)S(1)}, u32[]{:S(2)}, u32[]{:S(2)}) collective-permute-start(f32[19,8,128]{2,1,0:T(8,128)} %pack_cols.1), channel_id=1, source_target_pairs={{0,120},{8,0},{16,8},{24,16},{32,24},{40,32},{48,40},{56,48},{64,5... | collective-permute-start | bytes 233480 | tf_op jit(solution)/shard_map/ppermute | solution.py:652
  8.6 0.0 copy-done
  8.6 0.0 copy-done.1
  8.7 3.6 %own_cells.1 = (f32[19,3,64,128]{3,2,1,0:T(8,128)S(1)}, f32[2,9,4,8,128]{4,3,2,1,0:T(8,128)S(1)}, f32[8,128]{1,0:T(8,128)S(1)}, f32[40,384]{1,0:T(8,128)S(1)}, f32[40,384]{1,0:T(8,128)S(1)}) custom-call(s32[6,8,16]{2,1,0:T(8,128)S(1)} %bitcast.2, f32[4]{0:T(128)S(1)} %copy-done.1, f32[19,64,384]{2,1,0:T(8,128)} %pop_ref.1, s32[2,512,1536]{2,1,0:T(8,128)} %height_hbm.1, ...), custom_call_target="tpu_custom_call" | custom-call | flops 8000000 | bytes 8000000 | tf_op jit(solution)/shard_map/own_cells/pallas_call | solution.py:302
  12.3 0.0 collective-permute-done.right_ref
  12.3 0.1 pack_rows.1
  12.4 0.0 collective-permute-start.1
  12.4 0.5 collective-permute-start.2
  12.9 3.3 %inner_rows.1 = (f32[19,64,128]{2,1,0:T(8,128)S(1)}, f32[19,4,64,128]{3,2,1,0:T(8,128)S(1)}, f32[16,24,128]{2,1,0:T(8,128)S(1)}, f32[16,216,128]{2,1,0:T(8,128)}) custom-call(f32[19,3,64,128]{3,2,1,0:T(8,128)S(1)} %get-tuple-element.16.own_ref, f32[2,9,4,8,128]{4,3,2,1,0:T(8,128)S(1)} %get-tuple-element.17.gas_ref, ...), custom_call_target="tpu_custom_call" | custom-call | flops 8000000 | bytes 8000000 | tf_op jit(solution)/shard_map/inner_rows/pallas_call | solution.py:407
  16.2 0.0 collective-permute-done.1.below_ref
  16.2 0.1 collective-permute-done.2.above_ref
  16.3 2.5 %edge_rows.1 = f32[16,216,128]{2,1,0:T(8,128)} custom-call(f32[16,216,128]{2,1,0:T(8,128)} %get-tuple-element.19.message_in, f32[16,24,128]{2,1,0:T(8,128)S(1)} %get-tuple-element.20.halves_in, f32[19,3,64,128]{3,2,1,0:T(8,128)S(1)} %get-tuple-element.16.own_ref, f32[19,64,128]{2,1,0:T(8,128)S(1)} %get-tuple-element.21.post_ref, ...), custom_call_target="tpu_custom_call", output_to_operand_aliasing={{}: (0, {})} | custom-call | flops 8000000 | bytes 8000000 | tf_op jit(solution)/shard_map/edge_rows/pallas_call | solution.py:513
  18.8 5.7 %all-to-all-start = ((f32[16,216,128]{2,1,0:T(8,128)}), f32[16,216,128]{2,1,0:T(8,128)S(1)}, u32[]{:S(2)}, u32[]{:S(2)}) async-start(f32[16,216,128]{2,1,0:T(8,128)} %edge_rows.1), calls=%async_computation | async-start | bytes 3538944 | tf_op jit(solution)/shard_map/all_to_all | solution.py:662
  24.5 0.7 fusion.1
  25.2 0.1 copy.9
  25.3 0.1 reshape.25
  25.4 0.2 convert_reduce_fusion
  25.6 0.1 select_reduce_fusion
  25.7 0.1 concatenate.3.table_ref
  25.8 29.1 %all-to-all-done.in_ref = f32[16,216,128]{2,1,0:T(8,128)S(1)} async-done(((f32[16,216,128]{2,1,0:T(8,128)}), f32[16,216,128]{2,1,0:T(8,128)S(1)}, u32[]{:S(2)}, u32[]{:S(2)}) %all-to-all-start) | async-done | bytes 1769504 | tf_op jit(solution)/shard_map/all_to_all | solution.py:662
  54.9 1.5 %sort_blocks.1 = f32[16,144,128]{2,1,0:T(8,128)S(1)} custom-call(s32[320]{0:T(512)S(1)} %concatenate.3.table_ref, f32[16,216,128]{2,1,0:T(8,128)S(1)} %all-to-all-done.in_ref), custom_call_target="tpu_custom_call" | custom-call | tf_op jit(solution)/shard_map/sort_blocks/pallas_call | solution.py:570
  56.5 22.1 %all_to_all.10.in_ref = f32[16,144,128]{2,1,0:T(8,128)S(1)} all-to-all(f32[16,144,128]{2,1,0:T(8,128)S(1)} %sort_blocks.1), channel_id=1, replica_groups=mesh['gx'=16,'gy'=8] {'gx'}, dimensions={0} | all-to-all | bytes 2359296 | tf_op jit(solution)/shard_map/all_to_all | solution.py:664
  78.6 1.8 %restore.1 = f32[1,4,19,32,128]{4,3,2,1,0:T(8,128)} custom-call(s32[1]{0:T(128)} %bitcast.taken_ref, f32[16,144,128]{2,1,0:T(8,128)S(1)} %all_to_all.10.in_ref), custom_call_target="tpu_custom_call" | custom-call | tf_op jit(solution)/shard_map/restore/pallas_call | solution.py:620
  (3 shorter events, 0.1 us)
Async XLA Ops:
  0.0 8.6 %copy-start = (s32[8,16,6]{1,0,2:T(8,128)S(1)}, s32[8,16,6]{1,0,2:T(8,128)}, u32[]{:S(2)}) copy-start(s32[8,16,6]{1,0,2:T(8,128)} %param.9) | copy-start | bytes 9220
  0.0 8.6 %copy-start.1 = (f32[4]{0:T(128)S(1)}, f32[4]{0:T(128)}, u32[]{:S(2)}) copy-start(f32[4]{0:T(128)} %wet_ref.1) | copy-start | bytes 52
  2.1 10.2 %collective-permute-start = (f32[19,8,128]{2,1,0:T(8,128)}, f32[19,8,128]{2,1,0:T(8,128)S(1)}, u32[]{:S(2)}, u32[]{:S(2)}) collective-permute-start(f32[19,8,128]{2,1,0:T(8,128)} %pack_cols.1), channel_id=1, source_target_pairs={{0,120},{8,0},{16,8},{24,16},{32,24},{40,32},{48,40},{56,48},{64,5... | collective-permute-start | bytes 233480 | tf_op jit(solution)/shard_map/ppermute | solution.py:652
  12.4 3.8 %collective-permute-start.1 = (f32[40,512]{1,0:T(8,128)S(1)}, f32[40,512]{1,0:T(8,128)S(1)}, u32[]{:S(2)}, u32[]{:S(2)}) collective-permute-start(f32[40,512]{1,0:T(8,128)S(1)} %get-tuple-element.25), channel_id=1, source_target_pairs={{0,7},{1,0},{2,1},{3,2},{4,3},{5,4},{6,5},{7,6},{8,15},{9,8},{10,9... | collective-permute-start | bytes 245768 | tf_op jit(solution)/shard_map/ppermute | solution.py:657
  12.4 3.9 %collective-permute-start.2 = (f32[40,512]{1,0:T(8,128)S(1)}, f32[40,512]{1,0:T(8,128)S(1)}, u32[]{:S(2)}, u32[]{:S(2)}) collective-permute-start(f32[40,512]{1,0:T(8,128)S(1)} %get-tuple-element.26), channel_id=1, source_target_pairs={{0,1},{1,2},{2,3},{3,4},{4,5},{5,6},{6,7},{7,0},{8,9},{9,10},{10,1... | collective-permute-start | bytes 245768 | tf_op jit(solution)/shard_map/ppermute | solution.py:658
  18.8 36.1 %all-to-all-start = ((f32[16,216,128]{2,1,0:T(8,128)}), f32[16,216,128]{2,1,0:T(8,128)S(1)}, u32[]{:S(2)}, u32[]{:S(2)}) async-start(f32[16,216,128]{2,1,0:T(8,128)} %edge_rows.1), calls=%async_computation | async-start | bytes 3538944 | tf_op jit(solution)/shard_map/all_to_all | solution.py:662

commit v2 on v1

--- a/solution.py
+++ b/solution.py
@@ -55,6 +55,8 @@
 f32 = jnp.float32
 i32 = jnp.int32
 MIB = 1024 * 1024
+PACK_LIMIT = 52 * MIB
+OWN_LIMIT = 50 * MIB
 
 
 def params(limit=16 * MIB):
@@ -66,7 +68,7 @@
 SMEM_SPEC = pl.BlockSpec(memory_space=pltpu.SMEM)
 OWN_SHAPE = jax.ShapeDtypeStruct((Q, 3, ROWS, LANES), f32)
 TWO_SHAPE = jax.ShapeDtypeStruct((Q, 4, ROWS, LANES), f32)
-RIGHT_SHAPE = jax.ShapeDtypeStruct((Q, ROWS, LANES), f32)
+LEFT_SHAPE = jax.ShapeDtypeStruct((Q, ROWS, LANES), f32)
 EDGE_SHAPE = jax.ShapeDtypeStruct((2 * Q + 2, 4 * LANES), f32)
 MESSAGE_SHAPE = jax.ShapeDtypeStruct((NDEV, PIECE, LANES), f32)
 HALVES_SHAPE = jax.ShapeDtypeStruct((NDEV, 4 * BLK, LANES), f32)
@@ -125,46 +127,47 @@
 def shifted(load, c, shift, lane):
     if shift == 0:
         return load(c)
+    here = load(c)
     if shift > 0:
-        here = load(c)
-        if c > 0:
-            here = jnp.where(lane >= LANES - shift, load(c - 1), here)
+        if c != 3:
+            here = jnp.where(lane >= LANES - shift, load((c + 3) % 4), here)
         return pltpu.roll(here, shift, 1)
-    here = load(c)
-    if c < 3:
-        here = jnp.where(lane < -shift, load(c + 1), here)
+    if c != 2:
+        here = jnp.where(lane < -shift, load((c + 1) % 4), here)
     return pltpu.roll(here, LANES + shift, 1)
 
 
 def pull(load, i, c, lane, extra):
     cx, cy, cz = VELOCITY[i]
-    moved = shifted(lambda t: load(i, t, cy), c, 4 * cx + cz - extra, lane)
+    moved = shifted(lambda t: load(i, t, cy), c, 4 * cx + cz + extra, lane)
     if cz == 1:
-        wall = shifted(lambda t: load(OPPOSITE[i], t, 0), c, -extra, lane)
+        wall = shifted(lambda t: load(OPPOSITE[i], t, 0), c, extra, lane)
         moved = jnp.where(lane % CZ == 0, wall, moved)
     elif cz == -1:
         moved = jnp.where(lane % CZ == CZ - 1, jnp.float32(WEIGHTS[i]), moved)
     return moved
 
 
-def pack_cols_kernel(pop_ref, out_ref, buf, sem):
+def pack_cols_kernel(pop_hbm, out_ref, buf, sem):
     copies = []
     for g in range(GROUPS):
         rows = pl.ds(TILE * g, TILE)
         copies.append(
             pltpu.make_async_copy(
-                pop_ref.at[:, rows, pl.ds(0, LANES)], buf.at[:, rows, :], sem.at[g]
+                pop_hbm.at[:, rows, pl.ds(2 * LANES, LANES)], buf.at[:, rows, :], sem.at[g]
             )
         )
         copies[-1].start()
+    lane = lane_of()
     for copy in copies:
         copy.wait()
-    lane = lane_of()
     for i in range(Q):
-        packed = buf[i, 0:TILE, :]
+        packed = pltpu.roll(buf[i, 0:TILE, :], 16, 1)
         for g in range(1, GROUPS):
-            rolled = pltpu.roll(buf[i, TILE * g : TILE * (g + 1), :], 16 * g, 1)
-            packed = jnp.where(lane >= 16 * g, rolled, packed)
+            last = buf[i, TILE * g : TILE * (g + 1), :]
+            if g < GROUPS - 1:
+                last = pltpu.roll(last, 16 * (g + 1), 1)
+            packed = jnp.where(lane >= 16 * g, last, packed)
         out_ref[i] = packed
 
 
@@ -175,7 +178,7 @@
         out_specs=VMEM_SPEC,
         out_shape=jax.ShapeDtypeStruct((Q, TILE, LANES), f32),
         scratch_shapes=[pltpu.VMEM((Q, ROWS, LANES), f32), pltpu.SemaphoreType.DMA((GROUPS,))],
-        compiler_params=params(63 * MIB),
+        compiler_params=params(PACK_LIMIT),
         name="pack_cols",
     )(populations)
 
@@ -200,8 +203,9 @@
     gy, gx = (lax.axis_index("gy"), lax.axis_index("gx"))
     n_gy = height_hbm.shape[1] // ROWS
     n_x = height_hbm.shape[2] // LANES
-    first = (gx * (BXD * B)) // LANES
-    offset = gx * (BXD * B) - first * LANES
+    start = lax.rem(gx * (BXD * B) + n_x * LANES - 4, n_x * LANES)
+    first = start // LANES
+    offset = start - first * LANES
     second = lax.rem(first + 1, n_x)
     up_gy, down_gy = (lax.rem(gy + n_gy - 1, n_gy), lax.rem(gy + 1, n_gy))
     copies = []
@@ -238,7 +242,7 @@
     wide = 4 * LANES
     cell = lax.broadcasted_iota(i32, (2 * LANES, wide), 0)
     place = lax.broadcasted_iota(i32, (2 * LANES, wide), 1)
-    spread = (cell == offset + place // CZ).astype(f32)
+    spread = (cell == offset + 4 + place // CZ - jnp.where(place >= 3 * LANES, LANES, 0)).astype(f32)
 
     def widen(values):
         return jnp.dot(values.astype(f32), spread, preferred_element_type=f32)
@@ -246,10 +250,10 @@
     def active(row, col, j):
         return (owner_ref[j, row, col] >= 0).astype(f32)
 
-    next_gx = lax.rem(gx + 1, NDEV)
+    left_gx = lax.rem(gx + NDEV - 1, NDEV)
 
     def act_tile(row, by, c):
-        return active(row, gx, BXD * by + c) if c < BXD else active(row, next_gx, BXD * by)
+        return active(row, gx, BXD * by + c) if c < 3 else active(row, left_gx, BXD * by + 2)
 
     for copy in copies:
         copy.wait()
@@ -277,9 +281,12 @@
             here = jnp.where(sub_low, tall[low : low + TILE, cols], tall[high : high + TILE, cols])
             wall = jnp.where(sub_low, level[low : low + TILE, cols], level[high : high + TILE, cols])
             gas_ref[s, GROUPS, c] = jnp.where(depth < here * act, 0.0, wall)
-    packed = gas_ref[0, 0, 3]
+    packed = pltpu.roll(gas_ref[0, 0, 3], 16, 1)
     for g in range(1, GROUPS):
-        packed = jnp.where(lane >= 16 * g, pltpu.roll(gas_ref[0, g, 3], 16 * g, 1), packed)
+        tile = gas_ref[0, g, 3]
+        if g < GROUPS - 1:
+            tile = pltpu.roll(tile, 16 * (g + 1), 1)
+        packed = jnp.where(lane >= 16 * g, tile, packed)
     packed_ref[...] = packed
 
     def step(g, carry):
@@ -317,22 +324,22 @@
             pltpu.SemaphoreType.DMA((GROUPS,)),
             pltpu.SemaphoreType.DMA((12,)),
         ],
-        compiler_params=params(50 * MIB),
+        compiler_params=params(OWN_LIMIT),
         cost_estimate=pl.CostEstimate(flops=8_000_000, bytes_accessed=8_000_000, transcendentals=0),
         name="own_cells",
     )(owner, wetting, populations, heights, wall_class)
 
 
-def pack_rows_kernel(up_in, down_in, right_ref, up_ref, down_ref):
+def pack_rows_kernel(up_in, down_in, left_ref, up_ref, down_ref):
     up_ref[:, 0 : 3 * LANES] = up_in[...]
     down_ref[:, 0 : 3 * LANES] = down_in[...]
     for i in range(Q):
-        up_ref[2 * i : 2 * i + 2, 3 * LANES :] = right_ref[i, 0:2, :]
-        last = pltpu.roll(right_ref[i], 16, 1)
-        down_ref[2 * i : 2 * i + 2, 3 * LANES :] = last[TILE - 2 : TILE]
-
-
-def pack_rows(up, down, right):
+        first = pltpu.roll(left_ref[i], LANES - 16, 1)
+        up_ref[2 * i : 2 * i + 2, 3 * LANES :] = first[0:2]
+        down_ref[2 * i : 2 * i + 2, 3 * LANES :] = left_ref[i, TILE - 2 : TILE, :]
+
+
+def pack_rows(up, down, left):
     return pl.pallas_call(
         pack_rows_kernel,
         in_specs=[VMEM_SPEC] * 3,
@@ -340,7 +347,7 @@
         out_shape=[EDGE_SHAPE, EDGE_SHAPE],
         compiler_params=params(),
         name="pack_rows",
-    )(up, down, right)
+    )(up, down, left)
 
 
 def store_running(load, out_ref, halves_ref, by, rr, lane):
@@ -369,12 +376,12 @@
     return pltpu.make_async_copy(buf.at[:, rows, :], out_hbm.at[:, rows, :], sem.at[j])
 
 
-def inner_kernel(own_ref, gas_ref, packed_ref, right_ref, post_ref, two_ref, halves_ref, out_hbm, buf, sem):
+def inner_kernel(own_ref, gas_ref, packed_ref, left_ref, post_ref, two_ref, halves_ref, out_hbm, buf, sem):
     lane = lane_of()
-    out = collide([right_ref[i] for i in range(Q)], packed_ref[...])
+    out = collide([left_ref[i] for i in range(Q)], packed_ref[...])
     for i in range(Q):
         for g in range(GROUPS):
-            tile = out[i] if g == 0 else pltpu.roll(out[i], LANES - 16 * g, 1)
+            tile = out[i] if g == GROUPS - 1 else pltpu.roll(out[i], LANES - 16 * (g + 1), 1)
             post_ref[i, TILE * g : TILE * (g + 1), :] = tile
 
     def second(g, carry):
@@ -403,20 +410,21 @@
         copy.wait()
 
 
-def inner_part(own, gas, packed, right):
+def inner_part(own, gas, packed, left):
     return pl.pallas_call(
         inner_kernel,
         in_specs=[VMEM_SPEC] * 4,
         out_specs=[VMEM_SPEC, VMEM_SPEC, VMEM_SPEC, HBM_SPEC],
-        out_shape=[RIGHT_SHAPE, TWO_SHAPE, HALVES_SHAPE, MESSAGE_SHAPE],
+        out_shape=[LEFT_SHAPE, TWO_SHAPE, HALVES_SHAPE, MESSAGE_SHAPE],
         scratch_shapes=[pltpu.VMEM((NDEV, BLK * B, LANES), f32), pltpu.SemaphoreType.DMA((BLK,))],
         compiler_params=params(),
         cost_estimate=pl.CostEstimate(flops=8_000_000, bytes_accessed=8_000_000, transcendentals=0),
         name="inner_rows",
-    )(own, gas, packed, right)
+    )(own, gas, packed, left)
 
 
 def edge_kernel(
+    table_ref,
     message_in,
     halves_in,
     own_ref,
@@ -509,13 +517,13 @@
         copy.wait()
 
 
-def edge_part(message, halves, own, post, two, gas, below, above):
+def edge_part(table, message, halves, own, post, two, gas, below, above):
     return pl.pallas_call(
         edge_kernel,
-        in_specs=[HBM_SPEC] + [VMEM_SPEC] * 7,
+        in_specs=[SMEM_SPEC, HBM_SPEC] + [VMEM_SPEC] * 7,
         out_specs=HBM_SPEC,
         out_shape=MESSAGE_SHAPE,
-        input_output_aliases={0: 0},
+        input_output_aliases={1: 0},
         scratch_shapes=[
             pltpu.VMEM((Q, 4, TILE, LANES), f32),
             pltpu.VMEM((Q, 4, 3 * TILE, LANES), f32),
@@ -530,25 +538,26 @@
         compiler_params=params(),
         cost_estimate=pl.CostEstimate(flops=8_000_000, bytes_accessed=8_000_000, transcendentals=0),
         name="edge_rows",
-    )(message, halves, own, post, two, gas, below, above)
+    )(table, message, halves, own, post, two, gas, below, above)
 
 
 def sort_kernel(table_ref, in_ref, out_ref):
     lane = lane_of()
     sub_low = row_of() < 4
-    count = NDEV * CAP
 
     def receiver(d, carry):
         halves = []
         for k in range(CAP):
             n = d * CAP + k
-            valid = table_ref[n] >= 0
-            s, j = (table_ref[count + n], table_ref[2 * count + n])
-            ps, pj = (table_ref[3 * count + n], table_ref[4 * count + n])
+            code = table_ref[n]
+            valid = code >= 0
+            code = jnp.maximum(code, 0)
+            s, j = (code & 15, (code >> 4) & 7)
+            ns, nj = ((code >> 8) & 15, code >> 12)
             for t in range(4):
                 now = in_ref[s, pl.ds(pl.multiple_of(B * j + TILE * t, TILE), TILE), :]
-                before = in_ref[ps, pl.ds(pl.multiple_of(B * pj + TILE * t, TILE), TILE), :]
-                tile = pltpu.roll(jnp.where(lane >= 120, before, now), 8, 1)
+                after = in_ref[ns, pl.ds(pl.multiple_of(B * nj + TILE * t, TILE), TILE), :]
+                tile = pltpu.roll(jnp.where(lane < 8, after, now), LANES - 8, 1)
                 out_ref[d, B * k + TILE * t : B * k + TILE * (t + 1), :] = jnp.where(valid, tile, 0.0)
 
             def half(s, j):
@@ -556,7 +565,7 @@
                 tile = in_ref[s, pl.ds(pl.multiple_of(BLK * B + TILE * pair, TILE), TILE), :]
                 return jnp.where(j - 2 * pair == k % 2, tile, pltpu.roll(tile, 4, 0))
 
-            tile = pltpu.roll(jnp.where(lane >= 120, half(ps, pj), half(s, j)), 8, 1)
+            tile = pltpu.roll(jnp.where(lane < 8, half(ns, nj), half(s, j)), LANES - 8, 1)
             halves.append(jnp.where(valid, tile, 0.0))
         for pair in range(CAP // 2):
             at = CAP * B + TILE * pair
@@ -577,7 +586,7 @@
     )(table, arrived)
 
 
-def restore_kernel(taken_ref, in_ref, out_hbm, buf, sem):
+def restore_kernel(table_ref, in_ref, out_hbm, buf, sem):
     lane = lane_of()
     sub_low = row_of() < 4
     top = lane % CZ == CZ - 1
@@ -606,9 +615,10 @@
                 value = jnp.where(top, taken * jnp.float32(WEIGHTS[i]), value)
             buf[k, i, at, :] = value
 
+    me = lax.axis_index("gx")
     copies = [pltpu.make_async_copy(buf.at[k], out_hbm.at[0, k], sem.at[k]) for k in range(CAP)]
     for k in range(CAP):
-        taken = (taken_ref[0] > k).astype(f32)
+        taken = (table_ref[me * CAP + k] >= 0).astype(f32)
         for t in range(4):
             slot(k, taken, t)
         copies[k].start()
@@ -616,7 +626,7 @@
         copy.wait()
 
 
-def restore(taken, arrived):
+def restore(table, arrived):
     return pl.pallas_call(
         restore_kernel,
         in_specs=[SMEM_SPEC, VMEM_SPEC],
@@ -625,44 +635,47 @@
         scratch_shapes=[pltpu.VMEM((CAP, Q, B, LANES), f32), pltpu.SemaphoreType.DMA((CAP,))],
         compiler_params=params(),
         name="restore",
-    )(taken, arrived)
-
-
-def tables(owner, gy, gx):
+    )(table, arrived)
+
+
+def block_codes():
+    codes = []
+    for b in range(NDEV * BLK):
+        s, j = divmod(b, BLK)
+        edge = j % BXD == BXD - 1
+        ns, nj = ((s + 1) % NDEV, j - BXD + 1) if edge else (s, j + 1)
+        codes.append(s + (j << 4) + (ns << 8) + (nj << 12))
+    return np.array(codes, np.int32)
+
+
+def tables(owner, gy):
     flat = lax.dynamic_index_in_dim(owner, gy, 0, keepdims=False).reshape(-1)
     number = jnp.arange(NDEV * BLK)
     same = (flat[:, None] == flat[None, :]) & (number[None, :] < number[:, None])
     slot = jnp.sum(same.astype(i32), axis=1)
     target = jnp.where(flat >= 0, flat * CAP + slot, -1)
     hit = target[:, None] == jnp.arange(NDEV * CAP)[None, :]
-    table = jnp.max(jnp.where(hit, number[:, None], -1), axis=0).astype(i32)
-    block = jnp.maximum(table, 0)
-    s, j = (block // BLK, block % BLK)
-    at_edge = j % BXD == 0
-    before_s = jnp.where(at_edge, (s + NDEV - 1) % NDEV, s)
-    before_j = jnp.where(at_edge, j + BXD - 1, j - 1)
-    taken = jnp.sum((flat == gx).astype(i32)).reshape(1)
-    return (jnp.concatenate([table, s, j, before_s, before_j]), taken)
+    return jnp.max(jnp.where(hit, block_codes()[:, None], -1), axis=0).astype(i32)
 
 
 def local(populations, heights, wall_class, wetting, owner):
     gy = lax.axis_index("gy")
-    gx = lax.axis_index("gx")
     n_gy = lax.axis_size("gy")
-    right = lax.ppermute(pack_cols(populations), "gx", [(i, (i - 1) % NDEV) for i in range(NDEV)])
+    left = lax.ppermute(pack_cols(populations), "gx", [(i, (i + 1) % NDEV) for i in range(NDEV)])
     own, gas, packed, up, down = own_part(
         owner.transpose(2, 0, 1), wetting, populations, heights, wall_class
     )
-    up, down = pack_rows(up, down, right)
+    up, down = pack_rows(up, down, left)
+    up, owner = lax.optimization_barrier((up, owner))
     below = lax.ppermute(up, "gy", [(i, (i - 1) % n_gy) for i in range(n_gy)])
     above = lax.ppermute(down, "gy", [(i, (i + 1) % n_gy) for i in range(n_gy)])
-    post, two, halves, message = inner_part(own, gas, packed, right)
-    message = edge_part(message, halves, own, post, two, gas, below, above)
-    table, taken = tables(owner, gy, gx)
+    table = tables(owner, gy)
+    post, two, halves, message = inner_part(own, gas, packed, left)
+    message = edge_part(table, message, halves, own, post, two, gas, below, above)
     gathered = lax.all_to_all(message, "gx", split_axis=0, concat_axis=0, tiled=True)
     chosen = sort_blocks(table, gathered)
     arrived = lax.all_to_all(chosen, "gx", split_axis=0, concat_axis=0, tiled=True)
-    return restore(taken, arrived)
+    return restore(table, arrived)
 
 
 def solution(mesh):

time: 80.7 us -> 74.3 us (0.921)
  blocking collectives: 22.1 us -> 53.3 us
  waiting for transfers between devices: 29.2 us -> 4.35 us
  starting transfers between devices: 12.7 us -> 2.16 us
  Pallas kernels: 14.9 us -> 12.1 us
  local copies, waits for them, and re-layouts: 0.26 us -> 1.71 us
    all_to_all x0 -> x1, blocking collectives: none -> 31.2 us  [local(): lax.all_to_all(message, 'gx', split_axis=0, concat_axis=0, tiled=True)]
    all_to_all x1 -> x0, waiting for transfers between devices: 29.1 us -> none  [local(): lax.all_to_all(message, 'gx', split_axis=0, concat_axis=0, tiled=True)]
    all_to_all x1 -> x0, starting transfers between devices: 5.68 us -> none  [local(): lax.all_to_all(message, 'gx', split_axis=0, concat_axis=0, tiled=True)]
    ppermute x1, starting transfers between devices: 6.56 us -> 1.65 us  [local(): lax.ppermute(pack_cols(populations), 'gx', [(i, (i + 1) % NDEV) for i in...]
    ppermute x1, waiting for transfers between devices: 0.01 us -> 3.64 us  [local(): lax.ppermute(pack_cols(populations), 'gx', [(i, (i + 1) % NDEV) for i in...]
    pallas_call x1, Pallas kernels: 2.08 us -> 0.39 us  [pack_cols(): pl.pallas_call(pack_cols_kernel, in_specs=[HBM_SPEC], out_specs=VMEM_SPEC...]
    unnamed x4 -> x8, local copies, waits for them, and re-layouts: 0.01 us -> 1.52 us
  transfers between devices with their start and end apart: 4 -> 3, of which waited for: 2 -> 2; matrix products, arithmetic and copies ran while one was open for 2% -> 0% of each run, Pallas kernels for 9% -> 8%
where the time goes in v2:
time: 74.3 us; the launch traced here: 74.1 us
  blocking collectives  53.3 us (72%)
  Pallas kernels  12.1 us (16%)
  waiting for transfers between devices  4.35 us (6%)
  starting transfers between devices  2.16 us (3%)
  local copies, waits for them, and re-layouts  1.71 us (2%)
    all_to_all x1, blocking collectives, local(): lax.all_to_all(message, 'gx', split_axis=0, concat_axis=0, tiled=True)  31.2 us
    all_to_all x1, blocking collectives, local(): lax.all_to_all(chosen, 'gx', split_axis=0, concat_axis=0, tiled=True)  22.1 us
    ppermute x1, waiting for transfers between devices, local(): lax.ppermute(pack_cols(populations), 'gx', [(i, (i + 1) % NDEV) for i in...  3.64 us
    pallas_call x1, Pallas kernels, own_part(): pl.pallas_call(own_kernel, in_specs=[SMEM_SPEC, SMEM_SPEC, HBM_SPEC, HBM_...  3.62 us
    pallas_call x1, Pallas kernels, inner_part(): pl.pallas_call(inner_kernel, in_specs=[VMEM_SPEC] * 4, out_specs=[VMEM_SP...  2.53 us
    pallas_call x1, Pallas kernels, edge_part(): pl.pallas_call(edge_kernel, in_specs=[SMEM_SPEC, HBM_SPEC] + [VMEM_SPEC]...  2.23 us
    pallas_call x1, Pallas kernels, restore(): pl.pallas_call(restore_kernel, in_specs=[SMEM_SPEC, VMEM_SPEC], out_specs...  1.68 us
    ppermute x1, starting transfers between devices, local(): lax.ppermute(pack_cols(populations), 'gx', [(i, (i + 1) % NDEV) for i in...  1.65 us
  transfers between devices with their start and end apart: 3, of which 2 were waited for; matrix products, arithmetic and copies ran while one was open for 0% of the time, Pallas kernels for 8%

profile of v2, /device:TPU:6, one launch (start us, length us, event | category | flops | bytes accessed | tf_op | source)
XLA Modules:
  0.0 74.1 jit_solution(13746262578181812416)
XLA Ops:
  0.0 0.0 copy-start
  0.0 1.5 %copy-done = f32[19,64,384]{2,1,0:T(8,128)S(1)} copy-done((f32[19,64,384]{2,1,0:T(8,128)S(1)}, f32[19,64,384]{2,1,0:T(8,128)}, u32[]{:S(2)}) %copy-start) | copy-done | bytes 1867800
  1.5 0.0 copy-start.1
  1.5 0.0 copy-start.2
  1.5 0.4 pack_cols.1
  1.9 1.6 %collective-permute-start = (f32[19,8,128]{2,1,0:T(8,128)S(1)}, f32[19,8,128]{2,1,0:T(8,128)S(1)}, u32[]{:S(2)}, u32[]{:S(2)}) collective-permute-start(f32[19,8,128]{2,1,0:T(8,128)S(1)} %pack_cols.1), channel_id=1, source_target_pairs={{0,8},{8,16},{16,24},{24,32},{32,40},{40,48},{48,56},{56,64},{64,7... | collective-permute-start | bytes 233480 | tf_op jit(solution)/shard_map/ppermute | solution.py:664
  3.6 0.0 copy-done.1
  3.6 0.0 copy-done.2
  3.6 3.6 %own_cells.1 = (f32[19,3,64,128]{3,2,1,0:T(8,128)S(1)}, f32[2,9,4,8,128]{4,3,2,1,0:T(8,128)S(1)}, f32[8,128]{1,0:T(8,128)S(1)}, f32[40,384]{1,0:T(8,128)S(1)}, f32[40,384]{1,0:T(8,128)S(1)}) custom-call(s32[6,8,16]{2,1,0:T(8,128)S(1)} %bitcast.1, f32[4]{0:T(128)S(1)} %copy-done.2, f32[19,64,384]{2,1,0:T(8,128)} %pop_hbm.3, s32[2,512,1536]{2,1,0:T(8,128)} %height_hbm.1, ...), custom_call_target="tpu_custom_call" | custom-call | flops 8000000 | bytes 8000000 | tf_op jit(solution)/shard_map/own_cells/pallas_call | solution.py:309
  7.2 0.0 copy-start.3
  7.2 3.6 %collective-permute-done.left_ref = f32[19,8,128]{2,1,0:T(8,128)S(1)} collective-permute-done((f32[19,8,128]{2,1,0:T(8,128)S(1)}, f32[19,8,128]{2,1,0:T(8,128)S(1)}, u32[]{:S(2)}, u32[]{:S(2)}) %collective-permute-start) | collective-permute-done | bytes 77856 | tf_op jit(solution)/shard_map/ppermute | solution.py:664
  10.8 0.1 pack_rows.1
  11.0 0.1 copy.10
  11.0 0.1 reshape.21
  11.1 0.2 convert_reduce_fusion
  11.3 0.0 collective-permute-start.1
  11.4 0.5 collective-permute-start.2
  11.9 2.5 %inner_rows.1 = (f32[19,64,128]{2,1,0:T(8,128)S(1)}, f32[19,4,64,128]{3,2,1,0:T(8,128)S(1)}, f32[16,24,128]{2,1,0:T(8,128)S(1)}, f32[16,216,128]{2,1,0:T(8,128)S(1)}) custom-call(f32[19,3,64,128]{3,2,1,0:T(8,128)S(1)} %get-tuple-element.22.own_ref, f32[2,9,4,8,128]{4,3,2,1,0:T(8,128)S(1)} %get-tuple-element.23.gas_ref, ...), custom_call_target="tpu_custom_call" | custom-call | flops 8000000 | bytes 8000000 | tf_op jit(solution)/shard_map/inner_rows/pallas_call | solution.py:414
  14.4 0.0 copy-done.3
  14.4 0.1 select_reduce_fusion.table_ref
  14.5 0.0 collective-permute-done.1.below_ref
  14.5 0.7 collective-permute-done.2.above_ref
  15.2 2.2 %edge_rows.1 = f32[16,216,128]{2,1,0:T(8,128)S(1)} custom-call(s32[64]{0:T(128)S(1)} %select_reduce_fusion.table_ref, f32[16,216,128]{2,1,0:T(8,128)S(1)} %get-tuple-element.25.message_in, f32[16,24,128]{2,1,0:T(8,128)S(1)} %get-tuple-element.26.halves_in, f32[19,3,64,128]{3,2,1,0:T(8,128)S(1)} %get-tuple-element.22.own_ref, ...), custom_call_target="tpu_custom_call", output_to_operand_aliasing={{}: (1, {})} | custom-call | flops 8000000 | bytes 8000000 | tf_op jit(solution)/shard_map/edge_rows/pallas_call | solution.py:521
  17.5 31.2 %all_to_all.10.in_ref = f32[16,216,128]{2,1,0:T(8,128)S(1)} all-to-all(f32[16,216,128]{2,1,0:T(8,128)S(1)} %edge_rows.1), channel_id=1, replica_groups=mesh['gx'=16,'gy'=8] {'gx'}, dimensions={0} | all-to-all | bytes 3538944 | tf_op jit(solution)/shard_map/all_to_all | solution.py:675
  48.6 1.6 %sort_blocks.1 = f32[16,144,128]{2,1,0:T(8,128)S(1)} custom-call(s32[64]{0:T(128)S(1)} %select_reduce_fusion.table_ref, f32[16,216,128]{2,1,0:T(8,128)S(1)} %all_to_all.10.in_ref), custom_call_target="tpu_custom_call" | custom-call | tf_op jit(solution)/shard_map/sort_blocks/pallas_call | solution.py:579
  50.2 22.1 %all_to_all.11.in_ref = f32[16,144,128]{2,1,0:T(8,128)S(1)} all-to-all(f32[16,144,128]{2,1,0:T(8,128)S(1)} %sort_blocks.1), channel_id=1, replica_groups=mesh['gx'=16,'gy'=8] {'gx'}, dimensions={0} | all-to-all | bytes 2359296 | tf_op jit(solution)/shard_map/all_to_all | solution.py:677
  72.4 1.7 %restore.1 = f32[1,4,19,32,128]{4,3,2,1,0:T(8,128)} custom-call(s32[64]{0:T(128)S(1)} %select_reduce_fusion.table_ref, f32[16,144,128]{2,1,0:T(8,128)S(1)} %all_to_all.11.in_ref), custom_call_target="tpu_custom_call" | custom-call | tf_op jit(solution)/shard_map/restore/pallas_call | solution.py:630
  (2 shorter events, 0.0 us)
Async XLA Ops:
  0.0 1.5 %copy-start = (f32[19,64,384]{2,1,0:T(8,128)S(1)}, f32[19,64,384]{2,1,0:T(8,128)}, u32[]{:S(2)}) copy-start(f32[19,64,384]{2,1,0:T(8,128)} %pop_hbm.3) | copy-start | bytes 5603332
  1.5 2.0 %copy-start.1 = (s32[8,16,6]{1,0,2:T(8,128)S(1)}, s32[8,16,6]{1,0,2:T(8,128)}, u32[]{:S(2)}) copy-start(s32[8,16,6]{1,0,2:T(8,128)} %param.10) | copy-start | bytes 9220
  1.5 2.0 %copy-start.2 = (f32[4]{0:T(128)S(1)}, f32[4]{0:T(128)}, u32[]{:S(2)}) copy-start(f32[4]{0:T(128)} %wet_ref.1) | copy-start | bytes 52
  1.9 8.9 %collective-permute-start = (f32[19,8,128]{2,1,0:T(8,128)S(1)}, f32[19,8,128]{2,1,0:T(8,128)S(1)}, u32[]{:S(2)}, u32[]{:S(2)}) collective-permute-start(f32[19,8,128]{2,1,0:T(8,128)S(1)} %pack_cols.1), channel_id=1, source_target_pairs={{0,8},{8,16},{16,24},{24,32},{32,40},{40,48},{48,56},{56,64},{64,7... | collective-permute-start | bytes 233480 | tf_op jit(solution)/shard_map/ppermute | solution.py:664
  7.2 7.2 %copy-start.3 = (s32[96]{0:T(128)S(1)}, s32[96]{0:T(128)}, u32[]{:S(2)}) copy-start(s32[96]{0:T(128)} %constant.21) | copy-start | bytes 1156
  11.3 3.2 %collective-permute-start.1 = (f32[40,512]{1,0:T(8,128)S(1)}, f32[40,512]{1,0:T(8,128)S(1)}, u32[]{:S(2)}, u32[]{:S(2)}) collective-permute-start(f32[40,512]{1,0:T(8,128)S(1)} %get-tuple-element.29), channel_id=1, source_target_pairs={{0,7},{1,0},{2,1},{3,2},{4,3},{5,4},{6,5},{7,6},{8,15},{9,8},{10,9... | collective-permute-start | bytes 245768 | tf_op jit(solution)/shard_map/ppermute | solution.py:670
  11.4 3.9 %collective-permute-start.2 = (f32[40,512]{1,0:T(8,128)S(1)}, f32[40,512]{1,0:T(8,128)S(1)}, u32[]{:S(2)}, u32[]{:S(2)}) collective-permute-start(f32[40,512]{1,0:T(8,128)S(1)} %get-tuple-element.30), channel_id=1, source_target_pairs={{0,1},{1,2},{2,3},{3,4},{4,5},{5,6},{6,7},{7,0},{8,9},{9,10},{10,1... | collective-permute-start | bytes 245768 | tf_op jit(solution)/shard_map/ppermute | solution.py:671

commit v3 on v2

--- a/solution.py
+++ b/solution.py
@@ -137,11 +137,25 @@
     return pltpu.roll(here, LANES + shift, 1)
 
 
-def pull(load, i, c, lane, extra):
+def shifted_message(load, c, shift, lane):
+    if c != 2:
+        return shifted(load, c, shift, lane)
+    if shift == 0:
+        return jnp.where(lane >= LANES - 8, load(3), load(2))
+    if shift > 0:
+        here = jnp.where(lane >= LANES - 8 - shift, load(3), load(2))
+        here = jnp.where(lane >= LANES - shift, load(1), here)
+        return pltpu.roll(here, shift, 1)
+    here = jnp.where(lane >= LANES - 8 - shift, load(3), load(2))
+    here = jnp.where(lane < -shift, load(0), here)
+    return pltpu.roll(here, LANES + shift, 1)
+
+
+def pull(load, i, c, lane, move=shifted):
     cx, cy, cz = VELOCITY[i]
-    moved = shifted(lambda t: load(i, t, cy), c, 4 * cx + cz + extra, lane)
+    moved = move(lambda t: load(i, t, cy), c, 4 * cx + cz, lane)
     if cz == 1:
-        wall = shifted(lambda t: load(OPPOSITE[i], t, 0), c, extra, lane)
+        wall = move(lambda t: load(OPPOSITE[i], t, 0), c, 0, lane)
         moved = jnp.where(lane % CZ == 0, wall, moved)
     elif cz == -1:
         moved = jnp.where(lane % CZ == CZ - 1, jnp.float32(WEIGHTS[i]), moved)
@@ -353,9 +367,9 @@
 def store_running(load, out_ref, halves_ref, by, rr, lane):
     for c in range(3):
         j = BXD * by + c
-        tail = pull(load, TAIL, c, lane, 8)
+        tail = pull(load, TAIL, c, lane, shifted_message)
         for n, i in enumerate(SENT):
-            value = pull(load, i, c, lane, 8)
+            value = pull(load, i, c, lane, shifted_message)
             if i in CARRIERS:
                 back = 3 - CARRIERS.index(i)
                 value = jnp.where(lane % CZ == CZ - 1, pltpu.roll(tail, back, 1), value)
@@ -390,7 +404,7 @@
             return own_ref[i, c, rows, :] if c < 3 else post_ref[i, rows, :]
 
         for c in range(4):
-            out = collide([pull(load, i, c, lane, 0) for i in range(Q)], gas_ref[1, g, c])
+            out = collide([pull(load, i, c, lane) for i in range(Q)], gas_ref[1, g, c])
             for i in range(Q):
                 two_ref[i, c, pl.ds(pl.multiple_of(TILE * g, TILE), TILE), :] = out[i]
         return carry
@@ -481,13 +495,13 @@
         return jnp.where(sub_low, bottom[i, c, 16 - dy : 24 - dy, :], top[i, c, 8 - dy : 16 - dy, :])
 
     for c in range(4):
-        out = collide([pull(load_first, i, c, lane, 0) for i in range(Q)], gas_ref[1, 0, c])
+        out = collide([pull(load_first, i, c, lane) for i in range(Q)], gas_ref[1, 0, c])
         for i in range(Q):
             top_two[i, c, 16:24, :] = out[i]
-        out = collide([pull(load_last, i, c, lane, 0) for i in range(Q)], gas_ref[1, GROUPS - 1, c])
+        out = collide([pull(load_last, i, c, lane) for i in range(Q)], gas_ref[1, GROUPS - 1, c])
         for i in range(Q):
             bottom_two[i, c, 16:24, :] = out[i]
-        out = collide([pull(load_halo, i, c, lane, 0) for i in range(Q)], gas_ref[1, GROUPS, c])
+        out = collide([pull(load_halo, i, c, lane) for i in range(Q)], gas_ref[1, GROUPS, c])
         for i in range(Q):
             top_two[i, c, 8:16, :] = out[i]
             bottom_two[i, c, 24:32, :] = out[i]
@@ -548,24 +562,18 @@
     def receiver(d, carry):
         halves = []
         for k in range(CAP):
-            n = d * CAP + k
-            code = table_ref[n]
+            code = table_ref[d * CAP + k]
             valid = code >= 0
             code = jnp.maximum(code, 0)
-            s, j = (code & 15, (code >> 4) & 7)
-            ns, nj = ((code >> 8) & 15, code >> 12)
+            s, j, after_s = (code & 15, (code >> 4) & 7, code >> 8)
             for t in range(4):
-                now = in_ref[s, pl.ds(pl.multiple_of(B * j + TILE * t, TILE), TILE), :]
-                after = in_ref[ns, pl.ds(pl.multiple_of(B * nj + TILE * t, TILE), TILE), :]
-                tile = pltpu.roll(jnp.where(lane < 8, after, now), LANES - 8, 1)
+                rows = pl.ds(pl.multiple_of(B * j + TILE * t, TILE), TILE)
+                tile = jnp.where(lane >= LANES - 8, in_ref[after_s, rows, :], in_ref[s, rows, :])
                 out_ref[d, B * k + TILE * t : B * k + TILE * (t + 1), :] = jnp.where(valid, tile, 0.0)
-
-            def half(s, j):
-                pair = lax.shift_right_logical(j, 1)
-                tile = in_ref[s, pl.ds(pl.multiple_of(BLK * B + TILE * pair, TILE), TILE), :]
-                return jnp.where(j - 2 * pair == k % 2, tile, pltpu.roll(tile, 4, 0))
-
-            tile = pltpu.roll(jnp.where(lane < 8, half(ns, nj), half(s, j)), LANES - 8, 1)
+            pair = lax.shift_right_logical(j, 1)
+            rows = pl.ds(pl.multiple_of(BLK * B + TILE * pair, TILE), TILE)
+            tile = jnp.where(lane >= LANES - 8, in_ref[after_s, rows, :], in_ref[s, rows, :])
+            tile = jnp.where(j - 2 * pair == k % 2, tile, pltpu.roll(tile, 4, 0))
             halves.append(jnp.where(valid, tile, 0.0))
         for pair in range(CAP // 2):
             at = CAP * B + TILE * pair
@@ -642,9 +650,8 @@
     codes = []
     for b in range(NDEV * BLK):
         s, j = divmod(b, BLK)
-        edge = j % BXD == BXD - 1
-        ns, nj = ((s + 1) % NDEV, j - BXD + 1) if edge else (s, j + 1)
-        codes.append(s + (j << 4) + (ns << 8) + (nj << 12))
+        after = (s + 1) % NDEV if j % BXD == BXD - 1 else s
+        codes.append(s + (j << 4) + (after << 8))
     return np.array(codes, np.int32)
 
 

time: 74.3 us -> 71.7 us (0.965)
  blocking collectives: 53.3 us -> 51.5 us
  Pallas kernels: 12.1 us -> 11 us
    all_to_all x1, blocking collectives: 22.1 us -> 21.2 us  [local(): lax.all_to_all(chosen, 'gx', split_axis=0, concat_axis=0, tiled=True)]
    all_to_all x1, blocking collectives: 31.2 us -> 30.4 us  [local(): lax.all_to_all(message, 'gx', split_axis=0, concat_axis=0, tiled=True)]
where the time goes in v3:
time: 71.7 us; the launch traced here: 71.4 us
  blocking collectives  51.5 us (72%)
  Pallas kernels  11 us (15%)
  waiting for transfers between devices  4.66 us (6%)
  starting transfers between devices  2.16 us (3%)
  local copies, waits for them, and re-layouts  1.71 us (2%)
    all_to_all x1, blocking collectives, local(): lax.all_to_all(message, 'gx', split_axis=0, concat_axis=0, tiled=True)  30.4 us
    all_to_all x1, blocking collectives, local(): lax.all_to_all(chosen, 'gx', split_axis=0, concat_axis=0, tiled=True)  21.2 us
    ppermute x1, waiting for transfers between devices, local(): lax.ppermute(pack_cols(populations), 'gx', [(i, (i + 1) % NDEV) for i in...  3.64 us
    pallas_call x1, Pallas kernels, own_part(): pl.pallas_call(own_kernel, in_specs=[SMEM_SPEC, SMEM_SPEC, HBM_SPEC, HBM_...  3.62 us
    pallas_call x1, Pallas kernels, inner_part(): pl.pallas_call(inner_kernel, in_specs=[VMEM_SPEC] * 4, out_specs=[VMEM_SP...  2.21 us
    pallas_call x1, Pallas kernels, edge_part(): pl.pallas_call(edge_kernel, in_specs=[SMEM_SPEC, HBM_SPEC] + [VMEM_SPEC]...  1.88 us
    pallas_call x1, Pallas kernels, restore(): pl.pallas_call(restore_kernel, in_specs=[SMEM_SPEC, VMEM_SPEC], out_specs...  1.68 us
    ppermute x1, starting transfers between devices, local(): lax.ppermute(pack_cols(populations), 'gx', [(i, (i + 1) % NDEV) for i in...  1.65 us
  transfers between devices with their start and end apart: 3, of which 2 were waited for; matrix products, arithmetic and copies ran while one was open for 0% of the time, Pallas kernels for 8%

profile of v3, /device:TPU:6, one launch (start us, length us, event | category | flops | bytes accessed | tf_op | source)
XLA Modules:
  0.0 71.4 jit_solution(10791939976136279148)
XLA Ops:
  0.0 0.0 copy-start
  0.0 1.5 %copy-done = f32[19,64,384]{2,1,0:T(8,128)S(1)} copy-done((f32[19,64,384]{2,1,0:T(8,128)S(1)}, f32[19,64,384]{2,1,0:T(8,128)}, u32[]{:S(2)}) %copy-start) | copy-done | bytes 1867800
  1.5 0.0 copy-start.1
  1.5 0.0 copy-start.2
  1.5 0.4 pack_cols.1
  1.9 1.6 %collective-permute-start = (f32[19,8,128]{2,1,0:T(8,128)S(1)}, f32[19,8,128]{2,1,0:T(8,128)S(1)}, u32[]{:S(2)}, u32[]{:S(2)}) collective-permute-start(f32[19,8,128]{2,1,0:T(8,128)S(1)} %pack_cols.1), channel_id=1, source_target_pairs={{0,8},{8,16},{16,24},{24,32},{32,40},{40,48},{48,56},{56,64},{64,7... | collective-permute-start | bytes 233480 | tf_op jit(solution)/shard_map/ppermute | solution.py:671
  3.6 0.0 copy-done.1
  3.6 0.0 copy-done.2
  3.6 3.6 %own_cells.1 = (f32[19,3,64,128]{3,2,1,0:T(8,128)S(1)}, f32[2,9,4,8,128]{4,3,2,1,0:T(8,128)S(1)}, f32[8,128]{1,0:T(8,128)S(1)}, f32[40,384]{1,0:T(8,128)S(1)}, f32[40,384]{1,0:T(8,128)S(1)}) custom-call(s32[6,8,16]{2,1,0:T(8,128)S(1)} %bitcast.1, f32[4]{0:T(128)S(1)} %copy-done.2, f32[19,64,384]{2,1,0:T(8,128)} %pop_hbm.3, s32[2,512,1536]{2,1,0:T(8,128)} %height_hbm.1, ...), custom_call_target="tpu_custom_call" | custom-call | flops 8000000 | bytes 8000000 | tf_op jit(solution)/shard_map/own_cells/pallas_call | solution.py:323
  7.2 0.0 copy-start.3
  7.2 3.6 %collective-permute-done.left_ref = f32[19,8,128]{2,1,0:T(8,128)S(1)} collective-permute-done((f32[19,8,128]{2,1,0:T(8,128)S(1)}, f32[19,8,128]{2,1,0:T(8,128)S(1)}, u32[]{:S(2)}, u32[]{:S(2)}) %collective-permute-start) | collective-permute-done | bytes 77856 | tf_op jit(solution)/shard_map/ppermute | solution.py:671
  10.8 0.1 pack_rows.1
  11.0 0.1 copy.10
  11.0 0.1 reshape.21
  11.1 0.2 convert_reduce_fusion
  11.3 0.0 collective-permute-start.1
  11.4 0.5 collective-permute-start.2
  11.9 2.2 %inner_rows.1 = (f32[19,64,128]{2,1,0:T(8,128)S(1)}, f32[19,4,64,128]{3,2,1,0:T(8,128)S(1)}, f32[16,24,128]{2,1,0:T(8,128)S(1)}, f32[16,216,128]{2,1,0:T(8,128)S(1)}) custom-call(f32[19,3,64,128]{3,2,1,0:T(8,128)S(1)} %get-tuple-element.22.own_ref, f32[2,9,4,8,128]{4,3,2,1,0:T(8,128)S(1)} %get-tuple-element.23.gas_ref, ...), custom_call_target="tpu_custom_call" | custom-call | flops 8000000 | bytes 8000000 | tf_op jit(solution)/shard_map/inner_rows/pallas_call | solution.py:428
  14.1 0.0 copy-done.3
  14.1 0.1 select_reduce_fusion.table_ref
  14.2 0.0 collective-permute-done.1.below_ref
  14.2 1.0 %collective-permute-done.2.above_ref = f32[40,512]{1,0:T(8,128)S(1)} collective-permute-done((f32[40,512]{1,0:T(8,128)S(1)}, f32[40,512]{1,0:T(8,128)S(1)}, u32[]{:S(2)}, u32[]{:S(2)}) %collective-permute-start.2) | collective-permute-done | bytes 81952 | tf_op jit(solution)/shard_map/ppermute | solution.py:678
  15.2 1.9 %edge_rows.1 = f32[16,216,128]{2,1,0:T(8,128)S(1)} custom-call(s32[64]{0:T(128)S(1)} %select_reduce_fusion.table_ref, f32[16,216,128]{2,1,0:T(8,128)S(1)} %get-tuple-element.25.message_in, f32[16,24,128]{2,1,0:T(8,128)S(1)} %get-tuple-element.26.halves_in, f32[19,3,64,128]{3,2,1,0:T(8,128)S(1)} %get-tuple-element.22.own_ref, ...), custom_call_target="tpu_custom_call", output_to_operand_aliasing={{}: (1, {})} | custom-call | flops 8000000 | bytes 8000000 | tf_op jit(solution)/shard_map/edge_rows/pallas_call | solution.py:535
  17.1 30.4 %all_to_all.10.in_ref = f32[16,216,128]{2,1,0:T(8,128)S(1)} all-to-all(f32[16,216,128]{2,1,0:T(8,128)S(1)} %edge_rows.1), channel_id=1, replica_groups=mesh['gx'=16,'gy'=8] {'gx'}, dimensions={0} | all-to-all | bytes 3538944 | tf_op jit(solution)/shard_map/all_to_all | solution.py:682
  47.5 1.1 %sort_blocks.1 = f32[16,144,128]{2,1,0:T(8,128)S(1)} custom-call(s32[64]{0:T(128)S(1)} %select_reduce_fusion.table_ref, f32[16,216,128]{2,1,0:T(8,128)S(1)} %all_to_all.10.in_ref), custom_call_target="tpu_custom_call" | custom-call | tf_op jit(solution)/shard_map/sort_blocks/pallas_call | solution.py:587
  48.6 21.2 %all_to_all.11.in_ref = f32[16,144,128]{2,1,0:T(8,128)S(1)} all-to-all(f32[16,144,128]{2,1,0:T(8,128)S(1)} %sort_blocks.1), channel_id=1, replica_groups=mesh['gx'=16,'gy'=8] {'gx'}, dimensions={0} | all-to-all | bytes 2359296 | tf_op jit(solution)/shard_map/all_to_all | solution.py:684
  69.8 1.7 %restore.1 = f32[1,4,19,32,128]{4,3,2,1,0:T(8,128)} custom-call(s32[64]{0:T(128)S(1)} %select_reduce_fusion.table_ref, f32[16,144,128]{2,1,0:T(8,128)S(1)} %all_to_all.11.in_ref), custom_call_target="tpu_custom_call" | custom-call | tf_op jit(solution)/shard_map/restore/pallas_call | solution.py:638
  (2 shorter events, 0.0 us)
Async XLA Ops:
  0.0 1.5 %copy-start = (f32[19,64,384]{2,1,0:T(8,128)S(1)}, f32[19,64,384]{2,1,0:T(8,128)}, u32[]{:S(2)}) copy-start(f32[19,64,384]{2,1,0:T(8,128)} %pop_hbm.3) | copy-start | bytes 5603332
  1.5 2.0 %copy-start.1 = (s32[8,16,6]{1,0,2:T(8,128)S(1)}, s32[8,16,6]{1,0,2:T(8,128)}, u32[]{:S(2)}) copy-start(s32[8,16,6]{1,0,2:T(8,128)} %param.10) | copy-start | bytes 9220
  1.5 2.0 %copy-start.2 = (f32[4]{0:T(128)S(1)}, f32[4]{0:T(128)}, u32[]{:S(2)}) copy-start(f32[4]{0:T(128)} %wet_ref.1) | copy-start | bytes 52
  1.9 8.9 %collective-permute-start = (f32[19,8,128]{2,1,0:T(8,128)S(1)}, f32[19,8,128]{2,1,0:T(8,128)S(1)}, u32[]{:S(2)}, u32[]{:S(2)}) collective-permute-start(f32[19,8,128]{2,1,0:T(8,128)S(1)} %pack_cols.1), channel_id=1, source_target_pairs={{0,8},{8,16},{16,24},{24,32},{32,40},{40,48},{48,56},{56,64},{64,7... | collective-permute-start | bytes 233480 | tf_op jit(solution)/shard_map/ppermute | solution.py:671
  7.2 6.9 %copy-start.3 = (s32[96]{0:T(128)S(1)}, s32[96]{0:T(128)}, u32[]{:S(2)}) copy-start(s32[96]{0:T(128)} %constant.21) | copy-start | bytes 1156
  11.3 2.9 %collective-permute-start.1 = (f32[40,512]{1,0:T(8,128)S(1)}, f32[40,512]{1,0:T(8,128)S(1)}, u32[]{:S(2)}, u32[]{:S(2)}) collective-permute-start(f32[40,512]{1,0:T(8,128)S(1)} %get-tuple-element.29), channel_id=1, source_target_pairs={{0,7},{1,0},{2,1},{3,2},{4,3},{5,4},{6,5},{7,6},{8,15},{9,8},{10,9... | collective-permute-start | bytes 245768 | tf_op jit(solution)/shard_map/ppermute | solution.py:677
  11.4 3.9 %collective-permute-start.2 = (f32[40,512]{1,0:T(8,128)S(1)}, f32[40,512]{1,0:T(8,128)S(1)}, u32[]{:S(2)}, u32[]{:S(2)}) collective-permute-start(f32[40,512]{1,0:T(8,128)S(1)} %get-tuple-element.30), channel_id=1, source_target_pairs={{0,1},{1,2},{2,3},{3,4},{4,5},{5,6},{6,7},{7,0},{8,9},{9,10},{10,1... | collective-permute-start | bytes 245768 | tf_op jit(solution)/shard_map/ppermute | solution.py:678

commit v4 on v3

--- a/solution.py
+++ b/solution.py
@@ -50,7 +50,6 @@
 WEIGHTS = [1.0 / 3.0] + [1.0 / 18.0] * 6 + [1.0 / 36.0] * 12
 OPPOSITE = [0, 2, 1, 4, 3, 6, 5, 8, 7, 10, 9, 12, 11, 14, 13, 16, 15, 18, 17]
 CARRIERS = (6, 12, 13)
-FIXED_TOP = (6, 12, 13, 16)
 
 f32 = jnp.float32
 i32 = jnp.int32
@@ -71,6 +70,7 @@
 LEFT_SHAPE = jax.ShapeDtypeStruct((Q, ROWS, LANES), f32)
 EDGE_SHAPE = jax.ShapeDtypeStruct((2 * Q + 2, 4 * LANES), f32)
 MESSAGE_SHAPE = jax.ShapeDtypeStruct((NDEV, PIECE, LANES), f32)
+PART_SHAPE = jax.ShapeDtypeStruct((NDEV, BLK * 2 * TILE, LANES), f32)
 HALVES_SHAPE = jax.ShapeDtypeStruct((NDEV, 4 * BLK, LANES), f32)
 
 
@@ -364,7 +364,7 @@
     )(up, down, left)
 
 
-def store_running(load, out_ref, halves_ref, by, rr, lane):
+def store_running(load, out_ref, halves_ref, halves_at, by, rr, lane, start):
     for c in range(3):
         j = BXD * by + c
         tail = pull(load, TAIL, c, lane, shifted_message)
@@ -374,23 +374,20 @@
                 back = 3 - CARRIERS.index(i)
                 value = jnp.where(lane % CZ == CZ - 1, pltpu.roll(tail, back, 1), value)
             if n < NDEV:
-                out_ref[n, B * j + TILE * rr : B * j + TILE * (rr + 1), :] = value
+                at = start(j) + TILE * (rr % 2)
+                out_ref[n, at : at + TILE, :] = value
             else:
                 m = 8 * (n - NDEV) + 2 * rr
-                halves_ref[m, 4 * j : 4 * j + 4, :] = value[0:4]
-                halves_ref[m + 1, 4 * j : 4 * j + 4, :] = value[4:8]
+                at = halves_at + 4 * j
+                halves_ref[m, at : at + 4, :] = value[0:4]
+                halves_ref[m + 1, at : at + 4, :] = value[4:8]
 
 
 INNER = ((0, 2), (0, 3), (1, 0), (1, 1))
 OUTER = ((0, 0), (0, 1), (1, 2), (1, 3))
 
 
-def message_copy(buf, out_hbm, sem, j, start):
-    rows = pl.ds(B * j + start, 2 * TILE)
-    return pltpu.make_async_copy(buf.at[:, rows, :], out_hbm.at[:, rows, :], sem.at[j])
-
-
-def inner_kernel(own_ref, gas_ref, packed_ref, left_ref, post_ref, two_ref, halves_ref, out_hbm, buf, sem):
+def inner_kernel(own_ref, gas_ref, packed_ref, left_ref, post_ref, two_ref, halves_ref, part_ref):
     lane = lane_of()
     out = collide([left_ref[i] for i in range(Q)], packed_ref[...])
     for i in range(Q):
@@ -410,27 +407,26 @@
         return carry
 
     lax.fori_loop(1, GROUPS - 1, second, 0)
-    copies = []
     for by, rr in INNER:
         at = TILE * (4 * by + rr)
         store_running(
-            lambda i, c, dy: two_ref[i, c, at - dy : at - dy + TILE, :], buf, halves_ref, by, rr, lane
+            lambda i, c, dy: two_ref[i, c, at - dy : at - dy + TILE, :],
+            part_ref,
+            halves_ref,
+            0,
+            by,
+            rr,
+            lane,
+            lambda j: 2 * TILE * j,
         )
-        if rr % 2 == 1:
-            for c in range(3):
-                copies.append(message_copy(buf, out_hbm, sem, BXD * by + c, TILE * (rr - 1)))
-                copies[-1].start()
-    for copy in copies:
-        copy.wait()
 
 
 def inner_part(own, gas, packed, left):
     return pl.pallas_call(
         inner_kernel,
         in_specs=[VMEM_SPEC] * 4,
-        out_specs=[VMEM_SPEC, VMEM_SPEC, VMEM_SPEC, HBM_SPEC],
-        out_shape=[LEFT_SHAPE, TWO_SHAPE, HALVES_SHAPE, MESSAGE_SHAPE],
-        scratch_shapes=[pltpu.VMEM((NDEV, BLK * B, LANES), f32), pltpu.SemaphoreType.DMA((BLK,))],
+        out_specs=[VMEM_SPEC] * 4,
+        out_shape=[LEFT_SHAPE, TWO_SHAPE, HALVES_SHAPE, PART_SHAPE],
         compiler_params=params(),
         cost_estimate=pl.CostEstimate(flops=8_000_000, bytes_accessed=8_000_000, transcendentals=0),
         name="inner_rows",
@@ -438,31 +434,29 @@
 
 
 def edge_kernel(
-    table_ref,
-    message_in,
-    halves_in,
+    part_ref,
+    halves_ref,
     own_ref,
     post_ref,
     two_ref,
     gas_ref,
     below_ref,
     above_ref,
-    out_hbm,
+    out_ref,
     halo,
     top,
     bottom,
     top_two,
     bottom_two,
-    buf,
-    halves,
-    sem,
-    half_sem,
 ):
     lane = lane_of()
     sub_low = row_of() < 4
     tall = ROWS - TILE
 
-    halves[...] = halves_in[...]
+    out_ref[:, BLK * B :, :] = halves_ref[...]
+    for j in range(BLK):
+        at = B * j + (2 * TILE if j < BXD else 0)
+        out_ref[:, at : at + 2 * TILE, :] = part_ref[:, 2 * TILE * j : 2 * TILE * (j + 1), :]
     halo[...] = jnp.ones(halo.shape, f32)
     for i in range(Q):
         for c in range(4):
@@ -506,7 +500,6 @@
             top_two[i, c, 8:16, :] = out[i]
             bottom_two[i, c, 24:32, :] = out[i]
 
-    copies = []
     for by, rr in OUTER:
         g = 4 * by + rr
 
@@ -518,41 +511,28 @@
                 return bottom_two[i, c, at : at + TILE, :]
             return two_ref[i, c, TILE * g - dy : TILE * (g + 1) - dy, :]
 
-        store_running(load, buf, halves, by, rr, lane)
-        if rr % 2 == 1:
-            for c in range(3):
-                copies.append(message_copy(buf, out_hbm, sem, BXD * by + c, TILE * (rr - 1)))
-                copies[-1].start()
-    copies.append(
-        pltpu.make_async_copy(halves, out_hbm.at[:, pl.ds(BLK * B, 4 * BLK), :], half_sem)
-    )
-    copies[-1].start()
-    for copy in copies:
-        copy.wait()
-
-
-def edge_part(table, message, halves, own, post, two, gas, below, above):
+        store_running(
+            load, out_ref, out_ref, BLK * B, by, rr, lane, lambda j: B * j + 2 * TILE * (rr // 2)
+        )
+
+
+def edge_part(part, halves, own, post, two, gas, below, above):
     return pl.pallas_call(
         edge_kernel,
-        in_specs=[SMEM_SPEC, HBM_SPEC] + [VMEM_SPEC] * 7,
-        out_specs=HBM_SPEC,
+        in_specs=[VMEM_SPEC] * 8,
+        out_specs=VMEM_SPEC,
         out_shape=MESSAGE_SHAPE,
-        input_output_aliases={1: 0},
         scratch_shapes=[
             pltpu.VMEM((Q, 4, TILE, LANES), f32),
             pltpu.VMEM((Q, 4, 3 * TILE, LANES), f32),
             pltpu.VMEM((Q, 4, 4 * TILE, LANES), f32),
             pltpu.VMEM((Q, 4, 4 * TILE, LANES), f32),
             pltpu.VMEM((Q, 4, 4 * TILE, LANES), f32),
-            pltpu.VMEM((NDEV, BLK * B, LANES), f32),
-            pltpu.VMEM((NDEV, 4 * BLK, LANES), f32),
-            pltpu.SemaphoreType.DMA((BLK,)),
-            pltpu.SemaphoreType.DMA,
         ],
         compiler_params=params(),
         cost_estimate=pl.CostEstimate(flops=8_000_000, bytes_accessed=8_000_000, transcendentals=0),
         name="edge_rows",
-    )(table, message, halves, own, post, two, gas, below, above)
+    )(part, halves, own, post, two, gas, below, above)
 
 
 def sort_kernel(table_ref, in_ref, out_ref):
@@ -594,13 +574,13 @@
     )(table, arrived)
 
 
-def restore_kernel(table_ref, in_ref, out_hbm, buf, sem):
+def restore_kernel(in_ref, out_hbm, buf, sem):
     lane = lane_of()
     sub_low = row_of() < 4
     top = lane % CZ == CZ - 1
     place = lane % CZ
 
-    def slot(k, taken, t):
+    def slot(k, t):
         rows = slice(B * k + TILE * t, B * k + TILE * (t + 1))
         planes = {m: in_ref[m, rows, :] for m in range(NDEV)}
         pair = CAP * B + TILE * (k // 2)
@@ -613,37 +593,35 @@
                 a = pltpu.roll(a, 4, 0)
             planes[NDEV + p] = jnp.where(sub_low, a, b)
         at = slice(TILE * t, TILE * (t + 1))
-        last = taken * jnp.float32(WEIGHTS[TAIL])
+        inflow = planes[SENT.index(16)]
         parts = [pltpu.roll(planes[i], LANES - 3 + n, 1) for n, i in enumerate(CARRIERS)]
         tail = jnp.where(place == 0, parts[0], jnp.where(place == 1, parts[1], parts[2]))
-        buf[k, TAIL, at, :] = jnp.where(top, last, tail)
+        buf[k, TAIL, at, :] = jnp.where(top, inflow, tail)
         for n, i in enumerate(SENT):
             value = planes[n]
-            if i in FIXED_TOP:
-                value = jnp.where(top, taken * jnp.float32(WEIGHTS[i]), value)
+            if i in CARRIERS:
+                value = jnp.where(top, inflow * (WEIGHTS[i] / WEIGHTS[16]), value)
             buf[k, i, at, :] = value
 
-    me = lax.axis_index("gx")
     copies = [pltpu.make_async_copy(buf.at[k], out_hbm.at[0, k], sem.at[k]) for k in range(CAP)]
     for k in range(CAP):
-        taken = (table_ref[me * CAP + k] >= 0).astype(f32)
         for t in range(4):
-            slot(k, taken, t)
+            slot(k, t)
         copies[k].start()
     for copy in copies:
         copy.wait()
 
 
-def restore(table, arrived):
+def restore(arrived):
     return pl.pallas_call(
         restore_kernel,
-        in_specs=[SMEM_SPEC, VMEM_SPEC],
+        in_specs=[VMEM_SPEC],
         out_specs=HBM_SPEC,
         out_shape=jax.ShapeDtypeStruct((1, CAP, Q, B, LANES), f32),
         scratch_shapes=[pltpu.VMEM((CAP, Q, B, LANES), f32), pltpu.SemaphoreType.DMA((CAP,))],
         compiler_params=params(),
         name="restore",
-    )(table, arrived)
+    )(arrived)
 
 
 def block_codes():
@@ -677,12 +655,13 @@
     below = lax.ppermute(up, "gy", [(i, (i - 1) % n_gy) for i in range(n_gy)])
     above = lax.ppermute(down, "gy", [(i, (i + 1) % n_gy) for i in range(n_gy)])
     table = tables(owner, gy)
-    post, two, halves, message = inner_part(own, gas, packed, left)
-    message = edge_part(table, message, halves, own, post, two, gas, below, above)
+    post, two, halves, part = inner_part(own, gas, packed, left)
+    message = edge_part(part, halves, own, post, two, gas, below, above)
+    message, table = lax.optimization_barrier((message, table))
     gathered = lax.all_to_all(message, "gx", split_axis=0, concat_axis=0, tiled=True)
     chosen = sort_blocks(table, gathered)
     arrived = lax.all_to_all(chosen, "gx", split_axis=0, concat_axis=0, tiled=True)
-    return restore(table, arrived)
+    return restore(arrived)
 
 
 def solution(mesh):

time: 71.7 us -> 71.4 us (level)
  blocking collectives: 51.5 us -> 52.7 us
  Pallas kernels: 11 us -> 10 us
    pallas_call x2, Pallas kernels: 3.56 us -> 2.55 us  [the longest x1 1.41 us: edge_part(): pl.pallas_call(edge_kernel, in_specs=[VMEM_SPEC] * 8, out_specs=VMEM_SPEC...]
    all_to_all x1, blocking collectives: 21.2 us -> 21.9 us  [local(): lax.all_to_all(chosen, 'gx', split_axis=0, concat_axis=0, tiled=True)]
  transfers between devices with their start and end apart: 3 -> 3, of which waited for: 2 -> 2; matrix products, arithmetic and copies ran while one was open for 0% -> 1% of each run, Pallas kernels for 8% -> 8%
where the time goes in v4:
time: 71.4 us; the launch traced here: 71.2 us
  blocking collectives  52.7 us (74%)
  Pallas kernels  10 us (14%)
  waiting for transfers between devices  4.23 us (6%)
  starting transfers between devices  2.16 us (3%)
  local copies, waits for them, and re-layouts  1.7 us (2%)
    all_to_all x1, blocking collectives, local(): lax.all_to_all(message, 'gx', split_axis=0, concat_axis=0, tiled=True)  30.8 us
    all_to_all x1, blocking collectives, local(): lax.all_to_all(chosen, 'gx', split_axis=0, concat_axis=0, tiled=True)  21.9 us
    ppermute x1, waiting for transfers between devices, local(): lax.ppermute(pack_cols(populations), 'gx', [(i, (i + 1) % NDEV) for i in...  3.64 us
    pallas_call x1, Pallas kernels, own_part(): pl.pallas_call(own_kernel, in_specs=[SMEM_SPEC, SMEM_SPEC, HBM_SPEC, HBM_...  3.62 us
    pallas_call x1, Pallas kernels, inner_part(): pl.pallas_call(inner_kernel, in_specs=[VMEM_SPEC] * 4, out_specs=[VMEM_SP...  2.28 us
    ppermute x1, starting transfers between devices, local(): lax.ppermute(pack_cols(populations), 'gx', [(i, (i + 1) % NDEV) for i in...  1.65 us
    unnamed x8, local copies, waits for them, and re-layouts  1.52 us
  transfers between devices with their start and end apart: 3, of which 2 were waited for; matrix products, arithmetic and copies ran while one was open for 1% of the time, Pallas kernels for 8%

profile of v4, /device:TPU:6, one launch (start us, length us, event | category | flops | bytes accessed | tf_op | source)
XLA Modules:
  0.0 71.2 jit_solution(13007920191105486930)
XLA Ops:
  0.0 0.0 copy-start
  0.0 1.5 %copy-done = f32[19,64,384]{2,1,0:T(8,128)S(1)} copy-done((f32[19,64,384]{2,1,0:T(8,128)S(1)}, f32[19,64,384]{2,1,0:T(8,128)}, u32[]{:S(2)}) %copy-start) | copy-done | bytes 1867800
  1.5 0.0 copy-start.1
  1.5 0.0 copy-start.2
  1.5 0.4 pack_cols.1
  1.9 1.6 %collective-permute-start = (f32[19,8,128]{2,1,0:T(8,128)S(1)}, f32[19,8,128]{2,1,0:T(8,128)S(1)}, u32[]{:S(2)}, u32[]{:S(2)}) collective-permute-start(f32[19,8,128]{2,1,0:T(8,128)S(1)} %pack_cols.1), channel_id=1, source_target_pairs={{0,8},{8,16},{16,24},{24,32},{32,40},{40,48},{48,56},{56,64},{64,7... | collective-permute-start | bytes 233480 | tf_op jit(solution)/shard_map/ppermute | solution.py:649
  3.6 0.0 copy-done.1
  3.6 0.0 copy-done.2
  3.6 3.6 %own_cells.1 = (f32[19,3,64,128]{3,2,1,0:T(8,128)S(1)}, f32[2,9,4,8,128]{4,3,2,1,0:T(8,128)S(1)}, f32[8,128]{1,0:T(8,128)S(1)}, f32[40,384]{1,0:T(8,128)S(1)}, f32[40,384]{1,0:T(8,128)S(1)}) custom-call(s32[6,8,16]{2,1,0:T(8,128)S(1)} %bitcast.1, f32[4]{0:T(128)S(1)} %copy-done.2, f32[19,64,384]{2,1,0:T(8,128)} %pop_hbm.3, s32[2,512,1536]{2,1,0:T(8,128)} %height_hbm.1, ...), custom_call_target="tpu_custom_call" | custom-call | flops 8000000 | bytes 8000000 | tf_op jit(solution)/shard_map/own_cells/pallas_call | solution.py:323
  7.2 0.0 copy-start.3
  7.2 3.6 %collective-permute-done.left_ref = f32[19,8,128]{2,1,0:T(8,128)S(1)} collective-permute-done((f32[19,8,128]{2,1,0:T(8,128)S(1)}, f32[19,8,128]{2,1,0:T(8,128)S(1)}, u32[]{:S(2)}, u32[]{:S(2)}) %collective-permute-start) | collective-permute-done | bytes 77856 | tf_op jit(solution)/shard_map/ppermute | solution.py:649
  10.8 0.1 pack_rows.1
  10.9 0.0 collective-permute-start.1
  11.0 0.5 collective-permute-start.2
  11.5 0.1 copy.9
  11.6 0.1 reshape.21
  11.6 0.2 convert_reduce_fusion
  11.8 2.3 %inner_rows.1 = (f32[19,64,128]{2,1,0:T(8,128)S(1)}, f32[19,4,64,128]{3,2,1,0:T(8,128)S(1)}, f32[16,24,128]{2,1,0:T(8,128)S(1)}, f32[16,96,128]{2,1,0:T(8,128)S(1)}) custom-call(f32[19,3,64,128]{3,2,1,0:T(8,128)S(1)} %get-tuple-element.20.own_ref, f32[2,9,4,8,128]{4,3,2,1,0:T(8,128)S(1)} %get-tuple-element.21.gas_ref, ...), custom_call_target="tpu_custom_call" | custom-call | flops 8000000 | bytes 8000000 | tf_op jit(solution)/shard_map/inner_rows/pallas_call | solution.py:425
  14.1 0.0 copy-done.3
  14.1 0.1 select_reduce_fusion.table_ref
  14.2 0.0 collective-permute-done.1.below_ref
  14.3 0.6 collective-permute-done.2.above_ref
  14.8 1.4 %edge_rows.1 = f32[16,216,128]{2,1,0:T(8,128)S(1)} custom-call(f32[16,96,128]{2,1,0:T(8,128)S(1)} %get-tuple-element.23.part_ref, f32[16,24,128]{2,1,0:T(8,128)S(1)} %get-tuple-element.24.halves_ref, f32[19,3,64,128]{3,2,1,0:T(8,128)S(1)} %get-tuple-element.20.own_ref, f32[19,64,128]{2,1,0:T(8,128)S(1)} %get-tuple-element.25.post_ref, ...), custom_call_target="tpu_custom_call" | custom-call | flops 8000000 | bytes 8000000 | tf_op jit(solution)/shard_map/edge_rows/pallas_call | solution.py:520
  16.3 30.8 %all_to_all.10.in_ref = f32[16,216,128]{2,1,0:T(8,128)S(1)} all-to-all(f32[16,216,128]{2,1,0:T(8,128)S(1)} %edge_rows.1), channel_id=1, replica_groups=mesh['gx'=16,'gy'=8] {'gx'}, dimensions={0} | all-to-all | bytes 3538944 | tf_op jit(solution)/shard_map/all_to_all | solution.py:661
  47.0 1.1 %sort_blocks.1 = f32[16,144,128]{2,1,0:T(8,128)S(1)} custom-call(s32[64]{0:T(128)S(1)} %select_reduce_fusion.table_ref, f32[16,216,128]{2,1,0:T(8,128)S(1)} %all_to_all.10.in_ref), custom_call_target="tpu_custom_call" | custom-call | tf_op jit(solution)/shard_map/sort_blocks/pallas_call | solution.py:567
  48.1 21.9 %all_to_all.11.in_ref = f32[16,144,128]{2,1,0:T(8,128)S(1)} all-to-all(f32[16,144,128]{2,1,0:T(8,128)S(1)} %sort_blocks.1), channel_id=1, replica_groups=mesh['gx'=16,'gy'=8] {'gx'}, dimensions={0} | all-to-all | bytes 2359296 | tf_op jit(solution)/shard_map/all_to_all | solution.py:663
  70.0 1.1 %restore.1 = f32[1,4,19,32,128]{4,3,2,1,0:T(8,128)} custom-call(f32[16,144,128]{2,1,0:T(8,128)S(1)} %all_to_all.11.in_ref), custom_call_target="tpu_custom_call" | custom-call | tf_op jit(solution)/shard_map/restore/pallas_call | solution.py:616
  (2 shorter events, 0.0 us)
Async XLA Ops:
  0.0 1.5 %copy-start = (f32[19,64,384]{2,1,0:T(8,128)S(1)}, f32[19,64,384]{2,1,0:T(8,128)}, u32[]{:S(2)}) copy-start(f32[19,64,384]{2,1,0:T(8,128)} %pop_hbm.3) | copy-start | bytes 5603332
  1.5 2.0 %copy-start.1 = (s32[8,16,6]{1,0,2:T(8,128)S(1)}, s32[8,16,6]{1,0,2:T(8,128)}, u32[]{:S(2)}) copy-start(s32[8,16,6]{1,0,2:T(8,128)} %param.10) | copy-start | bytes 9220
  1.5 2.0 %copy-start.2 = (f32[4]{0:T(128)S(1)}, f32[4]{0:T(128)}, u32[]{:S(2)}) copy-start(f32[4]{0:T(128)} %wet_ref.1) | copy-start | bytes 52
  1.9 8.9 %collective-permute-start = (f32[19,8,128]{2,1,0:T(8,128)S(1)}, f32[19,8,128]{2,1,0:T(8,128)S(1)}, u32[]{:S(2)}, u32[]{:S(2)}) collective-permute-start(f32[19,8,128]{2,1,0:T(8,128)S(1)} %pack_cols.1), channel_id=1, source_target_pairs={{0,8},{8,16},{16,24},{24,32},{32,40},{40,48},{48,56},{56,64},{64,7... | collective-permute-start | bytes 233480 | tf_op jit(solution)/shard_map/ppermute | solution.py:649
  7.2 6.9 %copy-start.3 = (s32[96]{0:T(128)S(1)}, s32[96]{0:T(128)}, u32[]{:S(2)}) copy-start(s32[96]{0:T(128)} %constant.21) | copy-start | bytes 1156
  10.9 3.3 %collective-permute-start.1 = (f32[40,512]{1,0:T(8,128)S(1)}, f32[40,512]{1,0:T(8,128)S(1)}, u32[]{:S(2)}, u32[]{:S(2)}) collective-permute-start(f32[40,512]{1,0:T(8,128)S(1)} %get-tuple-element.30), channel_id=1, source_target_pairs={{0,7},{1,0},{2,1},{3,2},{4,3},{5,4},{6,5},{7,6},{8,15},{9,8},{10,9... | collective-permute-start | bytes 245768 | tf_op jit(solution)/shard_map/ppermute | solution.py:655
  11.0 3.9 %collective-permute-start.2 = (f32[40,512]{1,0:T(8,128)S(1)}, f32[40,512]{1,0:T(8,128)S(1)}, u32[]{:S(2)}, u32[]{:S(2)}) collective-permute-start(f32[40,512]{1,0:T(8,128)S(1)} %get-tuple-element.31), channel_id=1, source_target_pairs={{0,1},{1,2},{2,3},{3,4},{4,5},{5,6},{6,7},{7,0},{8,9},{9,10},{10,1... | collective-permute-start | bytes 245768 | tf_op jit(solution)/shard_map/ppermute | solution.py:656

commit v5 on v4

--- a/solution.py
+++ b/solution.py
@@ -560,7 +560,7 @@
             out_ref[d, at : at + TILE, :] = jnp.where(sub_low, halves[2 * pair], halves[2 * pair + 1])
         return carry
 
-    lax.fori_loop(0, NDEV, receiver, 0, unroll=4)
+    lax.fori_loop(0, NDEV, receiver, 0, unroll=NDEV)
 
 
 def sort_blocks(table, arrived):

time: 71.4 us -> 71.4 us (level)
  no operation moved by 1% of the time
where the time goes in v5:
time: 71.4 us; the launch traced here: 71.1 us
  blocking collectives  52.7 us (74%)
  Pallas kernels  9.97 us (14%)
  waiting for transfers between devices  4.23 us (6%)
  starting transfers between devices  2.16 us (3%)
  local copies, waits for them, and re-layouts  1.7 us (2%)
    all_to_all x1, blocking collectives, local(): lax.all_to_all(message, 'gx', split_axis=0, concat_axis=0, tiled=True)  30.8 us
    all_to_all x1, blocking collectives, local(): lax.all_to_all(chosen, 'gx', split_axis=0, concat_axis=0, tiled=True)  21.9 us
    ppermute x1, waiting for transfers between devices, local(): lax.ppermute(pack_cols(populations), 'gx', [(i, (i + 1) % NDEV) for i in...  3.64 us
    pallas_call x1, Pallas kernels, own_part(): pl.pallas_call(own_kernel, in_specs=[SMEM_SPEC, SMEM_SPEC, HBM_SPEC, HBM_...  3.62 us
    pallas_call x1, Pallas kernels, inner_part(): pl.pallas_call(inner_kernel, in_specs=[VMEM_SPEC] * 4, out_specs=[VMEM_SP...  2.28 us
    ppermute x1, starting transfers between devices, local(): lax.ppermute(pack_cols(populations), 'gx', [(i, (i + 1) % NDEV) for i in...  1.65 us
    unnamed x8, local copies, waits for them, and re-layouts  1.52 us
  transfers between devices with their start and end apart: 3, of which 2 were waited for; matrix products, arithmetic and copies ran while one was open for 1% of the time, Pallas kernels for 8%

profile of v5, /device:TPU:6, one launch (start us, length us, event | category | flops | bytes accessed | tf_op | source)
XLA Modules:
  0.0 71.1 jit_solution(1333432142609427807)
XLA Ops:
  0.0 0.0 copy-start
  0.0 1.5 %copy-done = f32[19,64,384]{2,1,0:T(8,128)S(1)} copy-done((f32[19,64,384]{2,1,0:T(8,128)S(1)}, f32[19,64,384]{2,1,0:T(8,128)}, u32[]{:S(2)}) %copy-start) | copy-done | bytes 1867800
  1.5 0.0 copy-start.1
  1.5 0.0 copy-start.2
  1.5 0.4 pack_cols.1
  1.9 1.6 %collective-permute-start = (f32[19,8,128]{2,1,0:T(8,128)S(1)}, f32[19,8,128]{2,1,0:T(8,128)S(1)}, u32[]{:S(2)}, u32[]{:S(2)}) collective-permute-start(f32[19,8,128]{2,1,0:T(8,128)S(1)} %pack_cols.1), channel_id=1, source_target_pairs={{0,8},{8,16},{16,24},{24,32},{32,40},{40,48},{48,56},{56,64},{64,7... | collective-permute-start | bytes 233480 | tf_op jit(solution)/shard_map/ppermute | solution.py:649
  3.6 0.0 copy-done.1
  3.6 0.0 copy-done.2
  3.6 3.6 %own_cells.1 = (f32[19,3,64,128]{3,2,1,0:T(8,128)S(1)}, f32[2,9,4,8,128]{4,3,2,1,0:T(8,128)S(1)}, f32[8,128]{1,0:T(8,128)S(1)}, f32[40,384]{1,0:T(8,128)S(1)}, f32[40,384]{1,0:T(8,128)S(1)}) custom-call(s32[6,8,16]{2,1,0:T(8,128)S(1)} %bitcast.1, f32[4]{0:T(128)S(1)} %copy-done.2, f32[19,64,384]{2,1,0:T(8,128)} %pop_hbm.3, s32[2,512,1536]{2,1,0:T(8,128)} %height_hbm.1, ...), custom_call_target="tpu_custom_call" | custom-call | flops 8000000 | bytes 8000000 | tf_op jit(solution)/shard_map/own_cells/pallas_call | solution.py:323
  7.2 0.0 copy-start.3
  7.2 3.6 %collective-permute-done.left_ref = f32[19,8,128]{2,1,0:T(8,128)S(1)} collective-permute-done((f32[19,8,128]{2,1,0:T(8,128)S(1)}, f32[19,8,128]{2,1,0:T(8,128)S(1)}, u32[]{:S(2)}, u32[]{:S(2)}) %collective-permute-start) | collective-permute-done | bytes 77856 | tf_op jit(solution)/shard_map/ppermute | solution.py:649
  10.8 0.1 pack_rows.1
  10.9 0.0 collective-permute-start.1
  11.0 0.5 collective-permute-start.2
  11.5 0.1 copy.9
  11.6 0.1 reshape.21
  11.6 0.2 convert_reduce_fusion
  11.8 2.3 %inner_rows.1 = (f32[19,64,128]{2,1,0:T(8,128)S(1)}, f32[19,4,64,128]{3,2,1,0:T(8,128)S(1)}, f32[16,24,128]{2,1,0:T(8,128)S(1)}, f32[16,96,128]{2,1,0:T(8,128)S(1)}) custom-call(f32[19,3,64,128]{3,2,1,0:T(8,128)S(1)} %get-tuple-element.20.own_ref, f32[2,9,4,8,128]{4,3,2,1,0:T(8,128)S(1)} %get-tuple-element.21.gas_ref, ...), custom_call_target="tpu_custom_call" | custom-call | flops 8000000 | bytes 8000000 | tf_op jit(solution)/shard_map/inner_rows/pallas_call | solution.py:425
  14.1 0.0 copy-done.3
  14.1 0.1 select_reduce_fusion.table_ref
  14.2 0.0 collective-permute-done.1.below_ref
  14.3 0.6 collective-permute-done.2.above_ref
  14.8 1.4 %edge_rows.1 = f32[16,216,128]{2,1,0:T(8,128)S(1)} custom-call(f32[16,96,128]{2,1,0:T(8,128)S(1)} %get-tuple-element.23.part_ref, f32[16,24,128]{2,1,0:T(8,128)S(1)} %get-tuple-element.24.halves_ref, f32[19,3,64,128]{3,2,1,0:T(8,128)S(1)} %get-tuple-element.20.own_ref, f32[19,64,128]{2,1,0:T(8,128)S(1)} %get-tuple-element.25.post_ref, ...), custom_call_target="tpu_custom_call" | custom-call | flops 8000000 | bytes 8000000 | tf_op jit(solution)/shard_map/edge_rows/pallas_call | solution.py:520
  16.3 30.8 %all_to_all.10.in_ref = f32[16,216,128]{2,1,0:T(8,128)S(1)} all-to-all(f32[16,216,128]{2,1,0:T(8,128)S(1)} %edge_rows.1), channel_id=1, replica_groups=mesh['gx'=16,'gy'=8] {'gx'}, dimensions={0} | all-to-all | bytes 3538944 | tf_op jit(solution)/shard_map/all_to_all | solution.py:661
  47.0 1.0 %sort_blocks.1 = f32[16,144,128]{2,1,0:T(8,128)S(1)} custom-call(s32[64]{0:T(128)S(1)} %select_reduce_fusion.table_ref, f32[16,216,128]{2,1,0:T(8,128)S(1)} %all_to_all.10.in_ref), custom_call_target="tpu_custom_call" | custom-call | tf_op jit(solution)/shard_map/sort_blocks/pallas_call | solution.py:567
  48.1 21.9 %all_to_all.11.in_ref = f32[16,144,128]{2,1,0:T(8,128)S(1)} all-to-all(f32[16,144,128]{2,1,0:T(8,128)S(1)} %sort_blocks.1), channel_id=1, replica_groups=mesh['gx'=16,'gy'=8] {'gx'}, dimensions={0} | all-to-all | bytes 2359296 | tf_op jit(solution)/shard_map/all_to_all | solution.py:663
  70.0 1.1 %restore.1 = f32[1,4,19,32,128]{4,3,2,1,0:T(8,128)} custom-call(f32[16,144,128]{2,1,0:T(8,128)S(1)} %all_to_all.11.in_ref), custom_call_target="tpu_custom_call" | custom-call | tf_op jit(solution)/shard_map/restore/pallas_call | solution.py:616
  (2 shorter events, 0.0 us)
Async XLA Ops:
  0.0 1.5 %copy-start = (f32[19,64,384]{2,1,0:T(8,128)S(1)}, f32[19,64,384]{2,1,0:T(8,128)}, u32[]{:S(2)}) copy-start(f32[19,64,384]{2,1,0:T(8,128)} %pop_hbm.3) | copy-start | bytes 5603332
  1.5 2.0 %copy-start.1 = (s32[8,16,6]{1,0,2:T(8,128)S(1)}, s32[8,16,6]{1,0,2:T(8,128)}, u32[]{:S(2)}) copy-start(s32[8,16,6]{1,0,2:T(8,128)} %param.10) | copy-start | bytes 9220
  1.5 2.0 %copy-start.2 = (f32[4]{0:T(128)S(1)}, f32[4]{0:T(128)}, u32[]{:S(2)}) copy-start(f32[4]{0:T(128)} %wet_ref.1) | copy-start | bytes 52
  1.9 8.9 %collective-permute-start = (f32[19,8,128]{2,1,0:T(8,128)S(1)}, f32[19,8,128]{2,1,0:T(8,128)S(1)}, u32[]{:S(2)}, u32[]{:S(2)}) collective-permute-start(f32[19,8,128]{2,1,0:T(8,128)S(1)} %pack_cols.1), channel_id=1, source_target_pairs={{0,8},{8,16},{16,24},{24,32},{32,40},{40,48},{48,56},{56,64},{64,7... | collective-permute-start | bytes 233480 | tf_op jit(solution)/shard_map/ppermute | solution.py:649
  7.2 6.9 %copy-start.3 = (s32[96]{0:T(128)S(1)}, s32[96]{0:T(128)}, u32[]{:S(2)}) copy-start(s32[96]{0:T(128)} %constant.21) | copy-start | bytes 1156
  10.9 3.3 %collective-permute-start.1 = (f32[40,512]{1,0:T(8,128)S(1)}, f32[40,512]{1,0:T(8,128)S(1)}, u32[]{:S(2)}, u32[]{:S(2)}) collective-permute-start(f32[40,512]{1,0:T(8,128)S(1)} %get-tuple-element.30), channel_id=1, source_target_pairs={{0,7},{1,0},{2,1},{3,2},{4,3},{5,4},{6,5},{7,6},{8,15},{9,8},{10,9... | collective-permute-start | bytes 245768 | tf_op jit(solution)/shard_map/ppermute | solution.py:655
  11.0 3.9 %collective-permute-start.2 = (f32[40,512]{1,0:T(8,128)S(1)}, f32[40,512]{1,0:T(8,128)S(1)}, u32[]{:S(2)}, u32[]{:S(2)}) collective-permute-start(f32[40,512]{1,0:T(8,128)S(1)} %get-tuple-element.31), channel_id=1, source_target_pairs={{0,1},{1,2},{2,3},{3,4},{4,5},{5,6},{6,7},{7,0},{8,9},{9,10},{10,1... | collective-permute-start | bytes 245768 | tf_op jit(solution)/shard_map/ppermute | solution.py:656
